TPU v7x, 512 devices: a whole 4x8x8 slice. The times are simulated.
512 devices in a mesh: tm: 64 (over z_hi, y, x), head: 8 (over z_lo, core).
Axes of the slice: x: 4, y: 8, z: 8 (z_hi: 2, z_lo: 4; z = z_hi * 4 + z_lo), core: 2. Of those that a mesh axis runs over, the one named last changes fastest.
Arguments:
- frames_in: bfloat16 [64, 1024, 1024], P('tm', 'head'), may hold values from -400 to 400
- in_weight: bfloat16 [1024, 5120], P('tm', 'head'), may hold values from -0.1875 to 0.1875
- out_weight: bfloat16 [1024, 1024], replicated, may hold values from -0.1875 to 0.1875
- block_ids: int32 [1024], replicated, may hold values from 0 to 15, as said below
- block_lists: int32 [16, 4], replicated, may hold values from 0 to 15, as said below
- decays: float32 [64, 16, 16], P('tm', 'head'), may hold values from 0.3 to 1
Outputs:
- layer_out: bfloat16 [64, 1024, 1024], P('tm', 'head')
Inputs may be any that keep to these rules, and one draw needn't show every extreme that they name: `block_ids`: each of the 16 block ids is held by exactly 64 tokens. `block_lists`: row g starts with g itself, followed by 4 - 1 further blocks, all different.
All inputs are finite; a program needn't handle non-finite values.
Results may differ from a plain program's by a relative error of at most 0.0069.
Values may be sent and summed in bfloat16 or wider, within the bound.
A program may use at most 128 MiB of HBM per device.

v0:
```python
import math

import jax
import jax.numpy as jnp
from jax import lax
from jax.sharding import PartitionSpec as P

HD = 64
N = 64
TOKS = 1024
NB = 16


epsilon = 1e-06


def carried_in(shard, axis, combine, identity):
    peers, index = (lax.axis_size(axis), lax.axis_index(axis))
    everything = jax.tree.map(lambda part: lax.all_gather(part, axis), shard)
    start = jax.tree.map(
        lambda part, zero: jnp.broadcast_to(jnp.asarray(zero, part.dtype), part.shape),
        shard,
        identity,
    )

    def step(k, before):
        reached = k < index
        new = combine(before, jax.tree.map(lambda part: part[k], everything))
        return jax.tree.map(lambda a, b: jnp.where(reached, a, b), new, before)

    return lax.fori_loop(0, peers, step, start)


def head_norm(values):
    wide = values.astype(jnp.float32)
    return (wide * lax.rsqrt(jnp.mean(wide * wide, axis=-1, keepdims=True) + epsilon)).astype(
        jnp.bfloat16
    )


def combine(earlier, after_it):
    return (earlier[0] * after_it[0], after_it[0][:, :, None] * earlier[1] + after_it[1])


def body(frames_in, in_weight, out_weight, block_ids, block_lists, decays):
    frame_count, local_tokens, feature_width = frames_in.shape
    heads_here = decays.shape[1]
    groups = decays.shape[2]
    tokens = block_ids.shape[0]
    block_size = tokens // groups
    head_size = HD
    state_size = N
    selected_count = block_lists.shape[1]
    inputs_wide = frames_in.astype(jnp.float32)
    normed = (
        inputs_wide
        * lax.rsqrt(jnp.mean(inputs_wide * inputs_wide, axis=-1, keepdims=True) + epsilon)
    ).astype(jnp.bfloat16)
    full_rows = lax.all_gather(in_weight, "tm", axis=0, tiled=True)
    flat_rows = normed.reshape(frame_count * local_tokens, feature_width)
    local_flat = jnp.dot(
        flat_rows,
        lax.all_gather(full_rows, "head", axis=1, tiled=True),
        preferred_element_type=jnp.float32,
    ).astype(jnp.bfloat16)
    local_proj = local_flat.reshape(frame_count, local_tokens, local_flat.shape[1])
    projected = lax.all_to_all(local_proj, "head", split_axis=2, concat_axis=1, tiled=True)
    projected = projected.reshape(frame_count, tokens, heads_here, 5, head_size)
    sort_order = jnp.argsort(block_ids, stable=True)
    inverse_order = jnp.argsort(sort_order, stable=True)
    sorted_proj = jnp.take(projected, sort_order, axis=1).reshape(
        frame_count, groups, block_size, heads_here, 5, head_size
    )
    queries = head_norm(sorted_proj[:, :, :, :, 0])
    key_rows = head_norm(sorted_proj[:, :, :, :, 1])
    values_sorted = sorted_proj[:, :, :, :, 2]
    map_sorted = sorted_proj[:, :, :, :, 3, :state_size]
    readers_sorted = sorted_proj[:, :, :, :, 4, :state_size].astype(jnp.float32)
    chosen_keys = jnp.take(key_rows, block_lists, axis=1).reshape(
        frame_count, groups, selected_count * block_size, heads_here, head_size
    )
    chosen_values = jnp.take(values_sorted, block_lists, axis=1).reshape(
        frame_count, groups, selected_count * block_size, heads_here, head_size
    )
    updates = jnp.einsum(
        "fgshn,fgshd->fhgnd", map_sorted, values_sorted, preferred_element_type=jnp.float32
    )
    local_state = jnp.zeros((heads_here, groups, state_size, head_size), jnp.float32)
    running = jnp.ones((heads_here, groups), jnp.float32)
    frame_at = 0
    local_state = decays[frame_at][:, :, None, None] * local_state + updates[frame_at]
    running = decays[frame_at] * running
    states = [local_state]
    products = [running]
    identity = (
        jnp.ones((heads_here, groups), jnp.float32),
        jnp.zeros((heads_here, groups, state_size * head_size), jnp.float32),
    )
    carried = carried_in(
        (running, local_state.reshape(heads_here, groups, state_size * head_size)),
        "tm",
        combine,
        identity,
    )
    incoming = carried[1].reshape(heads_here, groups, state_size, head_size)
    ssm_scale = 1.0 / (N * math.sqrt(TOKS // NB))
    frame_at = 0
    full_state = states[frame_at] + products[frame_at][:, :, None, None] * incoming
    readout_sorted = (
        jnp.einsum(
            "gshn,hgnd->gshd", readers_sorted[frame_at], full_state, precision=lax.Precision.HIGHEST
        )
        * ssm_scale
    )
    scores = jnp.einsum(
        "gshd,guhd->hgsu",
        queries[frame_at],
        chosen_keys[frame_at],
        preferred_element_type=jnp.float32,
    ) / math.sqrt(head_size)
    exponent = jnp.exp(scores)
    weights = (exponent / jnp.sum(exponent, axis=-1, keepdims=True)).astype(jnp.bfloat16)
    attended = jnp.einsum(
        "hgsu,guhd->gshd", weights, chosen_values[frame_at], preferred_element_type=jnp.float32
    )
    mixed_sorted = (
        (attended + readout_sorted).astype(jnp.bfloat16).reshape(tokens, heads_here * head_size)
    )
    frames_mixed = [jnp.take(mixed_sorted, inverse_order, axis=0)]
    mixed = jnp.stack(frames_mixed, axis=0)
    token_mix = lax.all_to_all(mixed, "head", split_axis=1, concat_axis=2, tiled=True)
    result = jnp.dot(
        token_mix.reshape(frame_count * local_tokens, token_mix.shape[2]),
        out_weight,
        preferred_element_type=jnp.float32,
    )
    return result.astype(jnp.bfloat16).reshape(frame_count, local_tokens, feature_width)


def solution(mesh):
    return jax.shard_map(
        body,
        mesh=mesh,
        in_specs=(P("tm", "head", None), P("tm", "head"), P(), P(), P(), P("tm", "head", None)),
        out_specs=P("tm", "head", None),
        check_vma=False,
    )
```

profile of v0, /device:TPU:1, one launch (start us, length us, event | category | flops | bytes accessed | tf_op | source)
XLA Modules:
  0.0 990.8 jit_solution(7445949897962662394)
XLA Ops:
  7.3 138.0 %all-gather.4.cloned.1.call-done = bf16[1024,640]{1,0:T(8,128)(2,1)} async-done(((bf16[16,640]{1,0:T(8,128)(2,1)}), bf16[1024,640]{1,0:T(8,128)(2,1)}) %all-gather.4.cloned.1.call-update) | async-done | bytes 1310736 | tf_op jit(solution)/shard_map/all_gather | solution.py:59
  146.4 112.3 %all-gather.6.cloned.1.call-done = bf16[1024,5120]{1,0:T(8,128)(2,1)} async-done(((bf16[1024,640]{1,0:T(8,128)(2,1)}), bf16[1024,5120]{1,0:T(8,128)(2,1)}) %all-gather.6.cloned.1.call-update) | async-done | bytes 10485776 | tf_op jit(solution)/shard_map/all_gather | solution.py:63
  258.7 5.7 fusion.1
  264.4 4.1 copy.51
  269.1 28.9 %reduce.4 = bf16[5120,128]{1,0:T(8,128)(2,1)S(1)} reduce(bf16[5120,1,128]{2,1,0:T(2,128)(2,1)} %bitcast.84, bf16[]{:T(256)} %broadcast.155), dimensions={1}, to_apply=%bitcast.66.reduce_sub_computation | reduce | bytes 2621442
  298.0 1.2 reshape.272
  299.2 6.9 all-to-all-start
  306.1 4.4 sort.31
  310.6 26.9 %all-to-all-done = bf16[8,2,40960]{2,1,0:T(2,128)(2,1)S(1)} async-done(((bf16[8,2,40960]{2,1,0:T(2,128)(2,1)}), bf16[8,2,40960]{2,1,0:T(2,128)(2,1)S(1)}, u32[]{:S(2)}, u32[]{:S(2)}) %all-to-all-start) | async-done | bytes 1310752 | tf_op jit(solution)/shard_map/all_to_all | solution.py:67
  337.5 3.7 reshape.273
  341.2 1.9 copy.73
  343.9 1.4 reshape.233
  345.4 6.2 copy.53
  351.6 13.9 %gather_fusion = bf16[1024,2,5,64]{3,1,2,0:T(2,128)(2,1)} fusion(bf16[1024,2,5,64]{3,1,2,0:T(2,128)(2,1)} %copy.53, s32[1024]{0:T(1024)S(1)} %fusion.28), kind=kCustom, calls=%fused_computation.2 | custom fusion | bytes 2625536 | tf_op jit(solution)/shard_map/jit(_take)/gather | solution.py:71
  365.4 2.1 copy.54
  367.9 1.4 copy-done.1
  370.9 1.9 broadcast_add_fusion
  373.2 4.4 sort.32
  377.6 194.0 %all_gather.14 = f32[64,2,16]{2,1,0:T(2,128)S(1)} all-gather(f32[1,2,16]{2,1,0:T(2,128)S(1)} %copy-done.4), channel_id=1, replica_groups=mesh['tm'=64,'head'=8] {'tm'}, dimensions={0}, use_global_device_ids=true | all-gather | bytes 8320 | tf_op jit(solution)/shard_map/all_gather | solution.py:19
  571.6 1.4 fusion.10
  573.0 1.4 fusion.17
  574.4 2.1 gather_fusion.3
  576.5 2.1 slice_bitcast_fusion
  578.5 2.2 gather_fusion.2
  580.7 4.7 broadcast_select_fusion.1
  585.4 4.3 copy.59
  589.7 4.3 squeeze_reshape.7
  594.0 4.3 copy.56
  598.3 4.3 squeeze_reshape.6
  602.6 1.5 fusion.9
  604.1 2.1 fusion.2
  606.3 1.7 fusion.13
  608.0 273.5 %all-gather.8.cloned.1.call-done = f32[64,2,16,4096]{3,2,1,0:T(8,128)} async-done(((f32[1,2,16,4096]{3,2,1,0:T(8,128)}), f32[64,2,16,4096]{3,2,1,0:T(8,128)}) %all-gather.8.cloned.1.call-update) | async-done | bytes 33554448 | tf_op jit(solution)/shard_map/all_gather | solution.py:19
  881.5 77.4 %while.14 = (s32[]{:T(128)}, f32[2,16,4096]{2,1,0:T(8,128)S(1)}, s32[]{:T(128)}, f32[64,2,16]{2,1,0:T(2,128)S(1)}, f32[64,2,16,4096]{3,2,1,0:T(8,128)}, /*index=5*/s32[]{:T(128)}, s32[]{:T(128)}) while((s32[]{:T(128)}, f32[2,16,4096]{2,1,0:T(8,128)S(1)}, s32[]{:T(128)}, f32[64,2,16]{2,1,0:T(2,128)S(1)}, ...), condition=%wide.region_7.9_spmd.clone, body=%wide.region_6.8_spmd.clone.sunk | while | flops 524292 | bytes 1573353 | solution.py:31
  882.7 1.2 fusion.35
  883.9 1.2 fusion.35
  885.1 1.2 fusion.35
  886.3 1.2 fusion.35
  887.5 1.2 fusion.35
  888.7 1.2 fusion.35
  889.9 1.2 fusion.35
  891.1 1.2 fusion.35
  892.3 1.2 fusion.35
  893.6 1.2 fusion.35
  894.8 1.2 fusion.35
  896.0 1.2 fusion.35
  897.2 1.2 fusion.35
  898.4 1.2 fusion.35
  899.6 1.2 fusion.35
  900.8 1.2 fusion.35
  902.0 1.2 fusion.35
  903.2 1.2 fusion.35
  904.4 1.2 fusion.35
  905.7 1.2 fusion.35
  906.9 1.2 fusion.35
  908.1 1.2 fusion.35
  909.3 1.2 fusion.35
  910.5 1.2 fusion.35
  958.9 1.4 reshape.207
  960.3 3.2 fusion.5
  964.2 3.2 gather_fusion.1
  968.0 2.3 reduce.5
  970.3 12.2 %all_to_all.30 = bf16[8,2,8192]{2,1,0:T(2,128)(2,1)S(1)} all-to-all(bf16[8,2,8192]{2,1,0:T(2,128)(2,1)S(1)} %reshape.274), channel_id=1, replica_groups=mesh['tm'=64,'head'=8] {'head'}, dimensions={0} | all-to-all | bytes 524288 | tf_op jit(solution)/shard_map/all_to_all | solution.py:131
  983.1 1.2 fusion.6
  (155 shorter events, 54.7 us)
Async XLA Ops:
  6.5 976.5 %copy-start = (bf16[1024,1024]{1,0:T(8,128)(2,1)S(1)}, bf16[1024,1024]{1,0:T(8,128)(2,1)}, u32[]{:S(2)}) copy-start(bf16[1024,1024]{1,0:T(8,128)(2,1)} %param.12) | copy-start | bytes 6291460
  6.5 138.8 %all-gather.4.cloned.1.call-start = ((), (), s32[]{:S(2)}) async-start(), calls=%async_computation.2 | async-start | bytes 1331200 | tf_op jit(solution)/shard_map/all_gather | solution.py:59
  7.3 251.5 %all-gather.6.cloned.1.call-start = ((), (), s32[]{:S(2)}) async-start(), calls=%async_computation.3 | async-start | bytes 11796480 | tf_op jit(solution)/shard_map/all_gather | solution.py:63
  298.0 8.2 copy-start.6
  298.0 12.6 %copy-start.4 = (f32[1,2,16]{2,1,0:T(2,128)S(1)}, f32[1,2,16]{2,1,0:T(2,128)}, u32[]{:S(2)}) copy-start(f32[1,2,16]{2,1,0:T(2,128)} %param.15) | copy-start | bytes 388
  299.2 38.3 %all-to-all-start = ((bf16[8,2,40960]{2,1,0:T(2,128)(2,1)}), bf16[8,2,40960]{2,1,0:T(2,128)(2,1)S(1)}, u32[]{:S(2)}, u32[]{:S(2)}) async-start(bf16[8,2,40960]{2,1,0:T(2,128)(2,1)} %reshape.272), calls=%async_computation | async-start | bytes 2621440 | tf_op jit(solution)/shard_map/all_to_all | solution.py:67
  306.1 575.3 %all-gather.8.cloned.1.call-start = ((), (), s32[]{:S(2)}) async-start(), calls=%async_computation.4 | async-start | bytes 34078720 | tf_op jit(solution)/shard_map/all_gather | solution.py:19
  367.9 1.4 copy-start.1
  369.7 3.1 copy-start.2
  369.7 3.1 copy-start.5
  602.6 3.6 copy-start.3
Sparse Core Ops, SparseCore 0:
  11.9 133.4 all-gather.3
  147.4 111.2 all-gather.5
  373.0 508.4 all-gather.7
where the time goes:
time: 995 us; the launch traced here: 991 us
  waiting for transfers between devices  551 us (55%)
  blocking collectives  206 us (21%)
  other arithmetic  127 us (13%)
  local copies, waits for them, and re-layouts  69.2 us (7%)
  matrix products  14.2 us (1%)
  between operations  13.4 us (1%)
    all_gather x1, waiting for transfers between devices, carried_in(): everything = jax.tree.map(lambda part: lax.all_gather(part, axis), shard)  273 us
    all_gather x1, blocking collectives, carried_in(): everything = jax.tree.map(lambda part: lax.all_gather(part, axis), shard)  194 us
    all_gather x1, waiting for transfers between devices, body(): full_rows = lax.all_gather(in_weight, 'tm', axis=0, tiled=True)  138 us
    all_gather x1, waiting for transfers between devices, body(): lax.all_gather(full_rows, 'head', axis=1, tiled=True)  112 us
    select_n x64, other arithmetic, step(): return jax.tree.map(lambda a, b: jnp.where(reached, a, b), new, before)  74.9 us
    unnamed x3, other arithmetic  31.2 us
    all_to_all x1, waiting for transfers between devices, body(): lax.all_to_all(local_proj, 'head', split_axis=2, concat_axis=1, tiled=True)  26.9 us
  transfers between devices with their start and end apart: 4, of which 4 were waited for; matrix products, arithmetic and copies ran while one was open for 5% of the time, Pallas kernels for 0%

commit v1 on v0

v1 whole, which is shorter than its diff:
```python
import functools

import jax
import jax.numpy as jnp
from jax import lax
from jax.experimental import pallas as pl
from jax.experimental.pallas import tpu as pltpu
from jax.sharding import PartitionSpec as P

HD = 64
NB = 16
D = 1024
TOKS = 1024
LOCAL = 128
WIDE = 2 * HD
NX, NY, NZ = 4, 8, 2
NG = NY * NZ
LINE, CORES = 4, 2
HEADS_AXIS = LINE * CORES
CHUNKS = 2
ROWS = 256
EPS = 1e-6
FAR = -256.0
F32, BF16 = jnp.float32, jnp.bfloat16
MESH = pl.DeviceIdType.MESH


def kernel(
    x_ref, w_ref, wo_hbm, bid_ref, lists_ref, dec_ref, out_ref,
    xbuf, wbuf, wo, bidb, fmat, qa, ka, va, cc, acc, res,
    sslab, ubuf, sx, tslab, tbuf, cslab, cbuf, stslab, sbuf, sbd, mslab, mbuf,
    dout, dxbuf, pdout, pdbuf,
    wz_s, wz_r, wx_s, wx_r, wy_s, wy_r, xg_s, xg_r, sib_s, sib_r,
    dx_s, dx_r, pd_s, pd_r, u_s, u_r, t_s, t_r, c_s, c_r, st_s, st_r, m_s, m_r, wo_sem,
):
    tm, head = lax.axis_index("tm"), lax.axis_index("head")
    x, r = lax.rem(tm, NX), lax.div(tm, NX)
    y, zh = lax.rem(r, NY), lax.div(r, NY)
    z, core = lax.div(head, CORES), lax.rem(head, CORES)

    def send(src, dst, ssem, rsem, tm_to, head_to):
        copy = pltpu.make_async_remote_copy(
            src_ref=src, dst_ref=dst, send_sem=ssem, recv_sem=rsem,
            device_id=(tm_to, head_to), device_id_type=MESH,
        )
        copy.start()
        return copy

    def tm_of(group, xx):
        return group * NX + xx

    barrier = pltpu.get_barrier_semaphore()
    for k in range(1, HEADS_AXIS):
        pl.semaphore_signal(
            barrier, inc=1, device_id=(tm, lax.rem(head + k, HEADS_AXIS)), device_id_type=MESH
        )
    for k in range(1, NX):
        pl.semaphore_signal(
            barrier, inc=1, device_id=(tm_of(r, lax.rem(x + k, NX)), head), device_id_type=MESH
        )
    for k in range(1, NG):
        pl.semaphore_signal(
            barrier, inc=1, device_id=(tm_of(lax.rem(r + k, NG), x), head), device_id_type=MESH
        )

    lane = lax.broadcasted_iota(jnp.int32, (1, WIDE), 1)
    low = lane < HD
    wo_copy = pltpu.make_async_copy(wo_hbm, wo, wo_sem)
    wo_copy.start()

    raw = [w_ref[:, i * WIDE:(i + 1) * WIDE].astype(F32) for i in range(5)]
    swap = functools.partial(pltpu.roll, shift=HD, axis=1)
    ordered = [
        jnp.where(low, raw[0], raw[2]),
        swap(jnp.where(low, raw[3], raw[0])),
        jnp.where(low, raw[1], raw[3]),
        swap(jnp.where(low, raw[4], raw[1])),
        jnp.where(low, raw[2], raw[4]),
    ]
    mine = wbuf.at[zh, y, x]
    for i in range(5):
        mine[:, i * WIDE:(i + 1) * WIDE] = ordered[i].astype(BF16)
    pl.semaphore_wait(barrier, HEADS_AXIS - 1 + NX - 1 + NG - 1)
    wz = send(mine, mine, wz_s, wz_r, tm_of((1 - zh) * NY + y, x), head)

    wide = x_ref[0].astype(F32)
    xbuf[head] = (
        wide * lax.rsqrt(jnp.mean(wide * wide, axis=-1, keepdims=True) + EPS)
    ).astype(BF16)
    per = LOCAL // CHUNKS

    def part(source, k):
        return xbuf.at[source * CORES + core, pl.ds(k * per, per)]

    def line_copy(way, s, k, source):
        to = z + 1 if way == 0 else z - 1
        return pltpu.make_async_remote_copy(
            src_ref=part(source, k), dst_ref=part(source, k),
            send_sem=xg_s.at[way, s - 1, k], recv_sem=xg_r.at[way, s - 1, k],
            device_id=(tm, to * CORES + core), device_id_type=MESH,
        )

    def has_next(way):
        return z < LINE - 1 if way == 0 else z > 0

    def source_sent(way, s):
        return z - (s - 1) if way == 0 else z + (s - 1)

    def is_source(zz):
        return (zz >= 0) & (zz < LINE)

    def send_line(way, s, k):
        source = source_sent(way, s)

        @pl.when(has_next(way) & is_source(source))
        def _():
            line_copy(way, s, k, source).start()

    def sib_copy(source, k):
        return pltpu.make_async_remote_copy(
            src_ref=part(source, k), dst_ref=part(source, k),
            send_sem=sib_s.at[source, k], recv_sem=sib_r.at[source, k],
            device_id=(tm, z * CORES + 1 - core), device_id_type=MESH,
        )

    def take_line(s, k):
        for way in range(2):
            source = z - s if way == 0 else z + s

            @pl.when(is_source(source))
            def _(way=way, source=source):
                line_copy(way, s, k, source).wait_recv()
                if s < LINE - 1:
                    send_line(way, s + 1, k)
                sib_copy(source, k).start()

    for k in range(CHUNKS):
        for way in range(2):
            send_line(way, 1, k)
    for k in range(CHUNKS):
        sib_copy(z, k).start()

    dec = dec_ref[0]
    gi = lax.broadcasted_iota(jnp.int32, (NB, NB), 0)
    gj = lax.broadcasted_iota(jnp.int32, (NB, NB), 1)
    cols = [
        jnp.sum(jnp.where(gi == gj, dec[h:h + 1, :], 0.0), axis=1, keepdims=True) for h in range(2)
    ]
    drow = jnp.where(low, cols[0], cols[1])
    dout[...] = jnp.zeros_like(dout)
    for j in range(NX):
        dout[j, 0:4, :] = drow[4 * j:4 * j + 4, :]
    dxbuf[x] = dout[x]

    wz.wait_recv()
    pair = wbuf.at[:, y, x]
    wx, dx = [], []
    for k in range(1, NX):
        j = lax.rem(x + k, NX)
        wx.append(send(pair, pair, wx_s.at[k - 1], wx_r.at[k - 1], tm_of(r, j), head))
        dx.append(send(dout.at[j], dxbuf.at[x], dx_s.at[k - 1], dx_r.at[k - 1], tm_of(r, j), head))
    for c in wx:
        c.wait_recv()

    def ring(way, s):
        step = s - 1 if s else 0
        held = lax.rem(y - step + NY, NY) if way == 0 else lax.rem(y + step, NY)
        to = lax.rem(y + 1, NY) if way == 0 else lax.rem(y + NY - 1, NY)
        ref = wbuf.at[:, held] if s < NY // 2 else wbuf.at[pl.ds(way, 1), held]
        return send(ref, ref, wy_s.at[way, s - 1], wy_r.at[way, s - 1], tm_of(zh * NY + to, x), head)

    rings = [[ring(0, 1), ring(1, 1)]]
    take_line(1, 0)

    for c in dx:
        c.wait_recv()
    prod = dxbuf[0]
    for i in range(1, NX):
        prod = prod * dxbuf[i]
    pdout[...] = prod
    pdbuf[r] = prod
    pd = []
    for k in range(1, NG):
        j = lax.rem(r + k, NG)
        pd.append(send(pdout, pdbuf.at[r], pd_s.at[k - 1], pd_r.at[k - 1], tm_of(j, x), head))
    take_line(1, 1)

    ids = jnp.broadcast_to(bid_ref[...].astype(F32), (WIDE, TOKS))
    for i in range(TOKS // WIDE):
        rows = pl.ds(i * WIDE, WIDE)
        bidb[rows, :] = ids[:, i * WIDE:(i + 1) * WIDE].T
    fmat[...] = jnp.zeros_like(fmat)
    wrapped = lane & (HD - 1)
    adjacent = jnp.zeros((NB, WIDE), jnp.bool_)
    for k in range(lists_ref.shape[1]):
        adjacent = adjacent | (lists_ref[:, k:k + 1] == wrapped)
    fmat[0:NB, :] = jnp.where(adjacent | (wrapped >= NB), 0.0, FAR).astype(BF16)

    for c in rings[0]:
        c.wait_recv()
    rings.append([ring(0, 2), ring(1, 2)])
    take_line(2, 0)
    take_line(2, 1)
    for c in rings[1]:
        c.wait_recv()
    rings.append([ring(0, 3), ring(1, 3)])
    take_line(3, 0)
    for c in rings[2]:
        c.wait_recv()
    rings.append([ring(0, 4), ring(1, 4)])
    take_line(3, 1)
    for zz in range(LINE):
        for k in range(CHUNKS):
            sib_copy(zz, k).wait_recv()
    for c in rings[3]:
        c.wait_recv()

    acc[...] = jnp.zeros_like(acc)
    weights = wbuf[...].reshape(D, 5 * WIDE)
    wrapped_f = wrapped.astype(F32)

    def normed_heads(values):
        square = values * values
        means = [
            jnp.sum(jnp.where(keep, square, 0.0), axis=-1, keepdims=True) * (1.0 / HD)
            for keep in (low, ~low)
        ]
        return (values * lax.rsqrt(jnp.where(low, means[0], means[1]) + EPS)).astype(BF16).astype(F32)

    def project(i, _):
        rows = pl.ds(pl.multiple_of(i * ROWS, ROWS), ROWS)
        tokens = xbuf[pl.ds(i * (ROWS // LOCAL), ROWS // LOCAL)].reshape(ROWS, D)
        p = jnp.dot(tokens, weights, preferred_element_type=F32).astype(BF16)
        q, k, v, b, c = (p[:, j * WIDE:(j + 1) * WIDE] for j in range(5))
        ids = bidb[rows, :]
        hot = jnp.where(ids == wrapped_f, 1.0, 0.0)
        banned = jnp.dot(hot.astype(BF16), fmat[...], preferred_element_type=F32)
        qn = normed_heads(q.astype(F32)) * 0.125
        kn = normed_heads(k.astype(F32))
        v32 = v.astype(F32)
        qa[0, rows, :] = jnp.where(low, qn, banned).astype(BF16)
        qa[1, rows, :] = jnp.where(low, banned, qn).astype(BF16)
        ka[0, rows, :] = jnp.where(low, kn, hot).astype(BF16)
        ka[1, rows, :] = jnp.where(low, hot, kn).astype(BF16)
        va[0, rows, :] = jnp.where(low, v32, 1.0).astype(BF16)
        va[1, rows, :] = jnp.where(low, 1.0, v32).astype(BF16)
        cc[rows, :] = c
        bt = b.astype(F32).T.astype(BF16)
        for g in range(0, NB, 4):
            masked = jnp.concatenate(
                [jnp.where(ids == float(g + n), v32, 0.0).astype(BF16) for n in range(4)], axis=1
            )
            at = slice(g * WIDE, (g + 4) * WIDE)
            acc[:, at] += jnp.dot(bt, masked, preferred_element_type=F32)
        return 0

    lax.fori_loop(0, TOKS // ROWS, project, 0)

    for g in range(NB):
        at = slice(g * WIDE, (g + 1) * WIDE)
        both = jnp.where(low, acc[0:HD, at], acc[HD:WIDE, at])
        sslab[g // 4, (g % 4) * HD:(g % 4 + 1) * HD, :] = both.astype(BF16)
    up = []
    for k in range(1, NX):
        j = lax.rem(x + k, NX)
        up.append(send(sslab.at[j], ubuf.at[x], u_s.at[k - 1], u_r.at[k - 1], tm_of(r, j), head))
    ubuf[x] = sslab[x]

    def attend(first, last):
        def one(n, _):
            h, i = lax.div(n, TOKS // ROWS), lax.rem(n, TOKS // ROWS)
            rows = pl.ds(pl.multiple_of(i * ROWS, ROWS), ROWS)
            score = lax.dot_general(
                qa[h, rows, :], ka[h], (((1,), (1,)), ((), ())), preferred_element_type=F32
            )
            res[h, rows, :] = jnp.dot(
                jnp.exp(score).astype(BF16), va[h], preferred_element_type=F32
            )
            return 0

        lax.fori_loop(first, last, one, 0)

    attend(0, 3)
    for c in up:
        c.wait_recv()
    blocks = NB // NX
    for g in range(blocks):
        at = slice(g * HD, (g + 1) * HD)
        state = ubuf[0, at, :].astype(F32)
        sx[0, at, :] = state
        for i in range(1, NX):
            state = dxbuf[i, g:g + 1, :] * state + ubuf[i, at, :].astype(F32)
            sx[i, at, :] = state
        for n in range(HD // NB):
            tslab[g * (HD // NB) + n] = state[n * NB:(n + 1) * NB, :].astype(BF16)
    tot = []
    for k in range(1, NG):
        j = lax.rem(r + k, NG)
        tot.append(send(tslab.at[j], tbuf.at[r], t_s.at[k - 1], t_r.at[k - 1], tm_of(j, x), head))
    tbuf[r] = tslab[r]
    attend(3, 5)
    for c in pd:
        c.wait_recv()
    for c in tot:
        c.wait_recv()
    carry = jnp.zeros((NB, WIDE), F32)
    own_block = pl.ds(lax.div(r, HD // NB), 1)
    for i in range(NG):
        cslab[i] = carry.astype(BF16)
        carry = pdbuf[i, own_block, :] * carry + tbuf[i].astype(F32)
    back = []
    for k in range(1, NG):
        j = lax.rem(r + k, NG)
        back.append(send(cslab.at[j], cbuf.at[r], c_s.at[k - 1], c_r.at[k - 1], tm_of(j, x), head))
    cbuf[r] = cslab[r]
    attend(5, 7)
    for c in back:
        c.wait_recv()
    for g in range(blocks):
        at = slice(g * HD, (g + 1) * HD)
        came = cbuf[g * (HD // NB):(g + 1) * (HD // NB)].reshape(HD, WIDE).astype(F32)
        for i in range(NX):
            came = dxbuf[i, g:g + 1, :] * came
            stslab[i, at, :] = (sx[i, at, :] + came).astype(BF16)
    states = []
    for k in range(1, NX):
        j = lax.rem(x + k, NX)
        states.append(
            send(stslab.at[j], sbuf.at[x], st_s.at[k - 1], st_r.at[k - 1], tm_of(r, j), head)
        )
    sbuf[x] = stslab[x]
    attend(7, 8)
    for c in states:
        c.wait_recv()
    for g in range(NB):
        state = sbuf[g // blocks, (g % blocks) * HD:(g % blocks + 1) * HD, :].astype(F32)
        sbd[g * WIDE:g * WIDE + HD, :] = jnp.where(low, state, 0.0).astype(BF16)
        sbd[g * WIDE + HD:(g + 1) * WIDE, :] = jnp.where(low, 0.0, state).astype(BF16)

    def mix(i, _):
        rows = pl.ds(pl.multiple_of(i * ROWS, ROWS), ROWS)
        ids = bidb[rows, :]
        c32 = cc[rows, :].astype(F32)
        spread = jnp.concatenate(
            [jnp.where(ids == float(g), c32, 0.0).astype(BF16) for g in range(NB)], axis=1
        )
        readout = jnp.dot(spread, sbd[...], preferred_element_type=F32) * (1.0 / 512.0)
        first, second = res[0, rows, :], res[1, rows, :]
        total = pltpu.roll(jnp.where(low, second, first), HD, 1)
        mixed = (jnp.where(low, first, second) / total + readout).astype(BF16)
        mslab[pl.ds(i * (ROWS // LOCAL), ROWS // LOCAL)] = mixed.reshape(
            ROWS // LOCAL, LOCAL, WIDE
        )
        return 0

    lax.fori_loop(0, TOKS // ROWS, mix, 0)
    sent = []
    for k in range(1, HEADS_AXIS):
        j = lax.rem(head + k, HEADS_AXIS)
        sent.append(send(mslab.at[j], mbuf.at[head], m_s.at[k - 1], m_r.at[k - 1], tm, j))
    mbuf[head] = mslab[head]
    wo_copy.wait()
    for c in sent:
        c.wait_recv()
    full = jnp.concatenate([mbuf[i] for i in range(HEADS_AXIS)], axis=1)
    out_ref[0] = jnp.dot(full, wo[...], preferred_element_type=F32).astype(BF16)

    for c in (wz, *wx, *dx, *pd, *up, *tot, *back, *states, *sent, *(c for p in rings for c in p)):
        c.wait_send()
    for k in range(CHUNKS):
        for s in range(1, LINE):
            for way in range(2):
                source = source_sent(way, s)

                @pl.when(has_next(way) & is_source(source))
                def _(way=way, s=s, k=k, source=source):
                    line_copy(way, s, k, source).wait_send()
        for zz in range(LINE):
            sib_copy(zz, k).wait_send()


def body(frames_in, in_weight, out_weight, block_ids, block_lists, decays):
    vmem = pl.BlockSpec(memory_space=pltpu.VMEM)
    dma = pltpu.SemaphoreType.DMA
    scratch = [
        pltpu.VMEM((HEADS_AXIS, LOCAL, D), BF16),
        pltpu.VMEM((NZ, NY, NX, 16, 5 * WIDE), BF16),
        pltpu.VMEM((D, D), BF16),
        pltpu.VMEM((TOKS, WIDE), F32),
        pltpu.VMEM((WIDE, WIDE), BF16),
        pltpu.VMEM((2, TOKS, WIDE), BF16),
        pltpu.VMEM((2, TOKS, WIDE), BF16),
        pltpu.VMEM((2, TOKS, WIDE), BF16),
        pltpu.VMEM((TOKS, WIDE), BF16),
        pltpu.VMEM((WIDE, NB * WIDE), F32),
        pltpu.VMEM((2, TOKS, WIDE), F32),
        pltpu.VMEM((NX, 256, WIDE), BF16),
        pltpu.VMEM((NX, 256, WIDE), BF16),
        pltpu.VMEM((NX, 256, WIDE), F32),
        pltpu.VMEM((NG, NB, WIDE), BF16),
        pltpu.VMEM((NG, NB, WIDE), BF16),
        pltpu.VMEM((NG, NB, WIDE), BF16),
        pltpu.VMEM((NG, NB, WIDE), BF16),
        pltpu.VMEM((NX, 256, WIDE), BF16),
        pltpu.VMEM((NX, 256, WIDE), BF16),
        pltpu.VMEM((NB * WIDE, WIDE), BF16),
        pltpu.VMEM((HEADS_AXIS, LOCAL, WIDE), BF16),
        pltpu.VMEM((HEADS_AXIS, LOCAL, WIDE), BF16),
        pltpu.VMEM((NX, 8, WIDE), F32),
        pltpu.VMEM((NX, 8, WIDE), F32),
        pltpu.VMEM((8, WIDE), F32),
        pltpu.VMEM((NG, 8, WIDE), F32),
        dma, dma, dma((NX - 1,)), dma((NX - 1,)), dma((2, 4)), dma((2, 4)),
        dma((2, LINE - 1, CHUNKS)), dma((2, LINE - 1, CHUNKS)),
        dma((LINE, CHUNKS)), dma((LINE, CHUNKS)),
        dma((NX - 1,)), dma((NX - 1,)), dma((NG - 1,)), dma((NG - 1,)),
        dma((NX - 1,)), dma((NX - 1,)), dma((NG - 1,)), dma((NG - 1,)),
        dma((NG - 1,)), dma((NG - 1,)), dma((NX - 1,)), dma((NX - 1,)),
        dma((HEADS_AXIS - 1,)), dma((HEADS_AXIS - 1,)), dma,
    ]
    return pl.pallas_call(
        kernel,
        out_shape=jax.ShapeDtypeStruct((1, LOCAL, D), BF16),
        in_specs=[vmem, vmem, pl.BlockSpec(memory_space=pl.ANY), vmem, vmem, vmem],
        out_specs=vmem,
        scratch_shapes=scratch,
        compiler_params=pltpu.CompilerParams(
            collective_id=0, has_side_effects=True, vmem_limit_bytes=56 * 1024 * 1024
        ),
        name="layer",
    )(frames_in, in_weight, out_weight, block_ids.reshape(1, TOKS), block_lists, decays)


def solution(mesh):
    return jax.shard_map(
        body,
        mesh=mesh,
        in_specs=(P("tm", "head", None), P("tm", "head"), P(), P(), P(), P("tm", "head", None)),
        out_specs=P("tm", "head", None),
        check_vma=False,
    )
```

time: 995 us -> 88.9 us (0.09)
  waiting for transfers between devices: 551 us -> 0 us
  blocking collectives: 206 us -> 0 us
  other arithmetic: 127 us -> 0 us
  Pallas kernels: 0 us -> 85.7 us
  local copies, waits for them, and re-layouts: 69.2 us -> 3.02 us
  matrix products: 14.2 us -> 0 us
  between operations: 13.4 us -> 0.01 us
    all_gather x3 -> x0, waiting for transfers between devices: 524 us -> none  [the longest x1 273 us: carried_in(): everything = jax.tree.map(lambda part: lax.all_gather(part, axis), shard)]
    all_gather x1 -> x0, blocking collectives: 194 us -> none  [carried_in(): everything = jax.tree.map(lambda part: lax.all_gather(part, axis), shard)]
    pallas_call x0 -> x1, Pallas kernels: none -> 85.7 us  [body(): pl.pallas_call(kernel, out_shape=jax.ShapeDtypeStruct((1, LOCAL, D), BF16...]
    select_n x68 -> x0, other arithmetic: 80.2 us -> none  [the longest x64 74.9 us: step(): return jax.tree.map(lambda a, b: jnp.where(reached, a, b), new, before)]
    unnamed x3 -> x0, other arithmetic: 31.2 us -> none
    all_to_all x1 -> x0, waiting for transfers between devices: 26.9 us -> none  [body(): lax.all_to_all(local_proj, 'head', split_axis=2, concat_axis=1, tiled=True)]
    gather x5 -> x0, local copies, waits for them, and re-layouts: 23.5 us -> none  [the longest x2 16 us: body(): jnp.take(projected, sort_order, axis=1)]
    dot_general x6 -> x0, matrix products: 14.2 us -> none  [the longest x1 5.65 us: body(): jnp.dot(flat_rows, lax.all_gather(full_rows, 'head', axis=1, tiled=True),...]
  transfers between devices with their start and end apart: 4 -> 0, of which waited for: 4 -> 0; matrix products, arithmetic and copies ran while one was open for 5% -> 0% of each run, Pallas kernels for 0% -> 0%
where the time goes in v1:
time: 88.9 us; the launch traced here: 88.7 us
  Pallas kernels  85.7 us (96%)
  local copies, waits for them, and re-layouts  3.02 us (3%)
    pallas_call x1, Pallas kernels, body(): pl.pallas_call(kernel, out_shape=jax.ShapeDtypeStruct((1, LOCAL, D), BF16...  85.7 us
    unnamed x2, local copies, waits for them, and re-layouts  3.02 us

profile of v1, /device:TPU:1, one launch (start us, length us, event | category | flops | bytes accessed | tf_op | source)
XLA Modules:
  0.0 88.7 jit_solution(14647236282305468263)
XLA Ops:
  0.0 1.4 %copy.7.lists_ref = s32[16,4]{1,0:T(8,128)} copy(s32[16,4]{0,1:T(4,128)} %param.10) | data formatting | bytes 512 | tf_op args[4]
  1.4 85.7 %layer.1 = bf16[1,128,1024]{2,1,0:T(8,128)(2,1)} custom-call(bf16[1,128,1024]{2,1,0:T(8,128)(2,1)} %x_ref.1, bf16[16,640]{1,0:T(8,128)(2,1)} %w_ref.1, bf16[1024,1024]{1,0:T(8,128)(2,1)} %wo_hbm.1, s32[1,1024]{1,0:T(1,128)} %bitcast.1, s32[16,4]{1,0:T(8,128)} %copy.7.lists_ref, f32[1,2,16]{2,1,0:T(2,128)} %dec_ref.1), custom_call_target="tpu_custom_call" | custom-call | tf_op jit(solution)/shard_map/layer/pallas_call | solution.py:421
  87.1 1.7 %copy.9 = bf16[1,128,1024]{2,1,0:T(8,128)(2,1)} copy(bf16[1,128,1024]{2,1,0:T(8,128)(2,1)} %layer.1) | data formatting | bytes 524288

commit v2 on v1

v2 whole, which is shorter than its diff:
```python
import functools

import jax
import jax.numpy as jnp
from jax import lax
from jax.experimental import pallas as pl
from jax.experimental.pallas import tpu as pltpu
from jax.sharding import PartitionSpec as P

HD = 64
NB = 16
D = 1024
TOKS = 1024
LOCAL = 128
WIDE = 2 * HD
NX, NY, NZ = 4, 8, 2
NG = NY * NZ
LINE, CORES = 4, 2
HEADS_AXIS = LINE * CORES
CHUNKS = 2
ROWS = 256
EPS = 1e-6
FAR = -256.0
F32, BF16 = jnp.float32, jnp.bfloat16
MESH = pl.DeviceIdType.MESH


class Move:
    def __init__(self, copy, go=None, come=None):
        self.copy, self.go, self.come, self.took = copy, go, come, False

    def start(self):
        self.copy.start() if self.go is None else pl.when(self.go)(self.copy.start)

    def wait_recv(self):
        self.took = True
        self.copy.wait_recv() if self.come is None else pl.when(self.come)(self.copy.wait_recv)

    def wait_send(self):
        self.copy.wait_send() if self.go is None else pl.when(self.go)(self.copy.wait_send)


def kernel(
    x_hbm, w_hbm, wo_hbm, bid_ref, lists_ref, dec_ref, out_ref,
    xin, win, xbuf, wbuf, wo, bidb, fmat, qa, ka, va, cc, acc, res,
    sslab, ubuf, sx, tslab, tbuf, cslab, cbuf, stslab, sbuf, sbd, mslab, mbuf,
    dout, dxbuf, pdout, pdbuf,
    wz_s, wz_r, wx_s, wx_r, wy_s, wy_r, xg_s, xg_r, sib_s, sib_r,
    dx_s, dx_r, pd_s, pd_r, u_s, u_r, t_s, t_r, c_s, c_r, st_s, st_r, m_s, m_r, in_sem,
):
    tm, head = lax.axis_index("tm"), lax.axis_index("head")
    x, r = lax.rem(tm, NX), lax.div(tm, NX)
    y, zh = lax.rem(r, NY), lax.div(r, NY)
    z, core = lax.div(head, CORES), lax.rem(head, CORES)

    def tm_at(zz, yy, xx):
        return (zz * NY + yy) * NX + xx

    barrier = pltpu.get_barrier_semaphore()

    def greet(tm_to, head_to):
        pl.semaphore_signal(barrier, inc=1, device_id=(tm_to, head_to), device_id_type=MESH)

    greet(tm_at(1 - zh, y, x), head)
    greet(tm_at(zh, y, lax.rem(x + 2, NX)), head)
    for k in (1, NX - 1):
        greet(tm_at(zh, y, lax.rem(x + k, NX)), head)
    for k in (1, NY - 1):
        greet(tm_at(zh, lax.rem(y + k, NY), x), head)
    pl.when(z > 0)(lambda: greet(tm, head - CORES))
    pl.when(z < LINE - 1)(lambda: greet(tm, head + CORES))
    greet(tm, z * CORES + 1 - core)
    expected = 7 + (z > 0).astype(jnp.int32) + (z < LINE - 1).astype(jnp.int32)

    loads = [
        pltpu.make_async_copy(src, dst, in_sem.at[i])
        for i, (src, dst) in enumerate(((w_hbm, win), (x_hbm, xin), (wo_hbm, wo)))
    ]
    for load in loads:
        load.start()
    wo_copy = loads[2]
    started = []

    def send(src, dst, ssem, rsem, tm_to, head_to, go=None, come=None):
        move = Move(
            pltpu.make_async_remote_copy(
                src_ref=src, dst_ref=dst, send_sem=ssem, recv_sem=rsem,
                device_id=(tm_to, head_to), device_id_type=MESH,
            ), go, come,
        )
        move.start()
        started.append(move)
        return move

    lane = lax.broadcasted_iota(jnp.int32, (1, WIDE), 1)
    low = lane < HD

    dec = dec_ref[0]
    gi = lax.broadcasted_iota(jnp.int32, (NB, NB), 0)
    gj = lax.broadcasted_iota(jnp.int32, (NB, NB), 1)
    cols = [
        jnp.sum(jnp.where(gi == gj, dec[h:h + 1, :], 0.0), axis=1, keepdims=True) for h in range(2)
    ]
    drow = jnp.where(low, cols[0], cols[1])
    dout[...] = jnp.zeros_like(dout)
    for j in range(NX):
        dout[j, 0:4, :] = drow[4 * j:4 * j + 4, :]
    dxbuf[x] = dout[x]

    loads[0].wait()
    raw = [win[:, i * WIDE:(i + 1) * WIDE].astype(F32) for i in range(5)]
    swap = functools.partial(pltpu.roll, shift=HD, axis=1)
    ordered = [
        jnp.where(low, raw[1], raw[3]),
        swap(jnp.where(low, raw[4], raw[1])),
        jnp.where(low, raw[0], raw[2]),
        swap(jnp.where(low, raw[3], raw[0])),
        jnp.where(low, raw[2], raw[4]),
    ]
    mine = wbuf.at[zh, y, x]
    for i in range(5):
        mine[:, i * WIDE:(i + 1) * WIDE] = ordered[i].astype(BF16)

    loads[1].wait()
    wide = xin[0].astype(F32)
    xbuf[head] = (
        wide * lax.rsqrt(jnp.mean(wide * wide, axis=-1, keepdims=True) + EPS)
    ).astype(BF16)
    per = LOCAL // CHUNKS

    def part(source, k):
        return xbuf.at[source * CORES + core, pl.ds(k * per, per)]

    def is_source(zz):
        return (zz >= 0) & (zz < LINE)

    line, sib = {}, {}

    def send_line(way, s, k):
        source, to = (z - (s - 1), z + 1) if way == 0 else (z + (s - 1), z - 1)
        come = is_source(z - s if way == 0 else z + s)
        ref = part(source, k)
        line[way, s, k] = send(
            ref, ref, xg_s.at[way, s - 1, k], xg_r.at[way, s - 1, k], tm, to * CORES + core,
            is_source(source) & is_source(to), come,
        )

    def send_sib(n, source, k, go=None, come=None):
        ref = part(source, k)
        sib[n, k] = send(
            ref, ref, sib_s.at[n, k], sib_r.at[n, k], tm, z * CORES + 1 - core, go, come
        )

    def take_line(s, k):
        for way in range(2):
            move = line[way, s, k]
            move.wait_recv()
            if s < LINE - 1:
                send_line(way, s + 1, k)
            send_sib(2 * s - 1 + way, z - s if way == 0 else z + s, k, move.come, move.come)

    def send_x(side):
        ref = wbuf.at[zh if side == 0 else 1 - zh, y, x]
        return [
            send(ref, ref, wx_s.at[side, k - 1], wx_r.at[side, k - 1],
                 tm_at(zh, y, lax.rem(x + k, NX)), head)
            for k in range(1, NX)
        ]

    def send_ring(side, s):
        half = zh if side == 0 else 1 - zh
        moves = []
        for way in range(2) if s < NY // 2 else (side,):
            held = lax.rem(y - (s - 1) + NY, NY) if way == 0 else lax.rem(y + (s - 1), NY)
            to = lax.rem(y + (1 if way == 0 else NY - 1), NY)
            ref = wbuf.at[half, held]
            moves.append(
                send(ref, ref, wy_s.at[side, way, s - 1], wy_r.at[side, way, s - 1],
                     tm_at(zh, to, x), head)
            )
        return moves

    def take(moves):
        for move in moves:
            move.wait_recv()

    pl.semaphore_wait(barrier, expected)
    wz = send(mine, mine, wz_s.at[0], wz_r.at[0], tm_at(1 - zh, y, x), head)
    own = send_x(0)
    for k in range(CHUNKS):
        for way in range(2):
            send_line(way, 1, k)
        send_sib(0, z, k)
    dx = []
    for k in range(1, NX):
        j = lax.rem(x + k, NX)
        dx.append(
            send(dout.at[j], dxbuf.at[x], dx_s.at[k - 1], dx_r.at[k - 1], tm_at(zh, y, j), head)
        )
    take(own)
    rings = {(0, 1): send_ring(0, 1)}

    ids = jnp.broadcast_to(bid_ref[...].astype(F32), (WIDE, TOKS))
    for i in range(TOKS // WIDE):
        bidb[i * WIDE:(i + 1) * WIDE, :] = ids[:, i * WIDE:(i + 1) * WIDE].T
    fmat[...] = jnp.zeros_like(fmat)
    wrapped = lane & (HD - 1)
    wrapped_f = wrapped.astype(F32)
    key_block = lax.broadcasted_iota(jnp.int32, (WIDE, NB), 0) & (HD - 1)
    adjacent = key_block >= NB
    for k in range(lists_ref.shape[0]):
        adjacent = adjacent | (lists_ref[k:k + 1, :] == key_block)
    fmat[:, 0:NB] = jnp.where(adjacent, 0.0, FAR).astype(BF16)
    acc[...] = jnp.zeros_like(acc)

    def forward(side, s):
        take(rings[side, s])
        if s < NY // 2:
            rings[side, s + 1] = send_ring(side, s + 1)

    take_line(1, 0)
    wz.wait_recv()
    other = send_x(1)
    forward(0, 1)
    take_line(1, 1)
    take(other)
    rings[1, 1] = send_ring(1, 1)
    forward(0, 2)
    take_line(2, 0)
    forward(1, 1)
    forward(0, 3)
    take(dx)
    prod = dxbuf[0]
    for i in range(1, NX):
        prod = prod * dxbuf[i]
    pdout[...] = prod
    pdbuf[zh, y] = prod
    take_line(2, 1)
    forward(1, 2)
    take_line(3, 0)
    forward(0, 4)
    forward(1, 3)
    take_line(3, 1)
    for move in sib.values():
        move.wait_recv()
    forward(1, 4)

    first_half, second_half = zh == 0, zh == 1

    def to_group(src_of, dst, ssem, rsem):
        moves = []
        for k in range(NY):
            j = lax.rem(y + k, NY)
            moves.append(
                send(src_of(j), dst.at[0, y], ssem.at[1, k], rsem.at[1, k], tm_at(1, j, x), head,
                     first_half, second_half)
            )
        for k in range(1, NY):
            j = lax.rem(y + k, NY)
            moves.append(
                send(src_of(j), dst.at[zh, y], ssem.at[0, k], rsem.at[0, k], tm_at(zh, j, x), head)
            )
        return moves

    def project_vb(i, _):
        rows = pl.ds(pl.multiple_of(i * ROWS, ROWS), ROWS)
        tokens = xbuf[pl.ds(i * (ROWS // LOCAL), ROWS // LOCAL)].reshape(ROWS, D)
        weights = wbuf[:, :, :, :, 0:2 * WIDE].reshape(D, 2 * WIDE)
        p = jnp.dot(tokens, weights, preferred_element_type=F32).astype(BF16).astype(F32)
        v, b = p[:, 0:WIDE], p[:, WIDE:2 * WIDE]
        ids = bidb[rows, :]
        va[0, rows, :] = jnp.where(low, v, 1.0).astype(BF16)
        va[1, rows, :] = jnp.where(low, 1.0, v).astype(BF16)
        bt = b.T.astype(BF16)
        for g in range(0, NB, 4):
            masked = jnp.concatenate(
                [jnp.where(ids == float(g + n), v, 0.0).astype(BF16) for n in range(4)], axis=1
            )
            at = slice(g * WIDE, (g + 4) * WIDE)
            acc[:, at] += jnp.dot(bt, masked, preferred_element_type=F32)
        return 0

    lax.fori_loop(0, TOKS // ROWS, project_vb, 0)
    for g in range(NB):
        at = slice(g * WIDE, (g + 1) * WIDE)
        both = jnp.where(low, acc[0:HD, at], acc[HD:WIDE, at])
        sslab[g // 4, (g % 4) * HD:(g % 4 + 1) * HD, :] = both.astype(BF16)
    up = []
    for k in (2, 1, 3):
        j = lax.rem(x + k, NX)
        up.append(
            send(sslab.at[j], ubuf.at[x], u_s.at[k - 1], u_r.at[k - 1], tm_at(zh, y, j), head)
        )
    ubuf[x] = sslab[x]
    pd = to_group(lambda j: pdout, pdbuf, pd_s, pd_r)

    def normed_heads(values):
        square = values * values
        means = [
            jnp.sum(jnp.where(keep, square, 0.0), axis=-1, keepdims=True) * (1.0 / HD)
            for keep in (low, ~low)
        ]
        return (values * lax.rsqrt(jnp.where(low, means[0], means[1]) + EPS)).astype(BF16).astype(F32)

    def project_qkc(i, _):
        rows = pl.ds(pl.multiple_of(i * ROWS, ROWS), ROWS)
        tokens = xbuf[pl.ds(i * (ROWS // LOCAL), ROWS // LOCAL)].reshape(ROWS, D)
        weights = wbuf[:, :, :, :, 2 * WIDE:].reshape(D, 3 * WIDE)
        p = jnp.dot(tokens, weights, preferred_element_type=F32).astype(BF16)
        q, k, c = (p[:, j * WIDE:(j + 1) * WIDE] for j in range(3))
        hot = jnp.where(bidb[rows, :] == wrapped_f, 1.0, 0.0)
        banned = lax.dot_general(
            hot.astype(BF16), fmat[...], (((1,), (1,)), ((), ())), preferred_element_type=F32
        )
        qn = normed_heads(q.astype(F32)) * 0.125
        kn = normed_heads(k.astype(F32))
        qa[0, rows, :] = jnp.where(low, qn, banned).astype(BF16)
        qa[1, rows, :] = jnp.where(low, banned, qn).astype(BF16)
        ka[0, rows, :] = jnp.where(low, kn, hot).astype(BF16)
        ka[1, rows, :] = jnp.where(low, hot, kn).astype(BF16)
        cc[rows, :] = c
        return 0

    lax.fori_loop(0, TOKS // ROWS, project_qkc, 0)

    def attend(first, last):
        def one(n, _):
            h, i = lax.div(n, TOKS // ROWS), lax.rem(n, TOKS // ROWS)
            rows = pl.ds(pl.multiple_of(i * ROWS, ROWS), ROWS)
            score = lax.dot_general(
                qa[h, rows, :], ka[h], (((1,), (1,)), ((), ())), preferred_element_type=F32
            )
            res[h, rows, :] = jnp.dot(
                jnp.exp(score).astype(BF16), va[h], preferred_element_type=F32
            )
            return 0

        lax.fori_loop(first, last, one, 0)

    attend(0, 2)
    take(up)
    blocks, owned = NB // NX, 32
    for g in range(blocks):
        at = slice(g * HD, (g + 1) * HD)
        state = ubuf[0, at, :].astype(F32)
        sx[0, at, :] = state
        for i in range(1, NX):
            state = dxbuf[i, g:g + 1, :] * state + ubuf[i, at, :].astype(F32)
            sx[i, at, :] = state
        for n in range(HD // owned):
            piece = state[n * owned:(n + 1) * owned, :].astype(BF16)
            tslab[g * (HD // owned) + n] = piece
    tot = to_group(lambda j: tslab.at[j], tbuf, t_s, t_r)
    tbuf[zh, y] = tslab[y]
    attend(2, 6)
    take(pd)
    take(tot)
    own_block = pl.ds(lax.div(y, HD // owned), 1)
    before = jnp.zeros((owned, WIDE), F32)
    for i in range(NY):
        before = pdbuf[0, i, own_block, :] * before + tbuf[0, i].astype(F32)
    carry = before * zh.astype(F32)
    for i in range(NY):
        cslab[i] = carry.astype(BF16)
        carry = pdbuf[zh, i, own_block, :] * carry + tbuf[zh, i].astype(F32)
    back = []
    for k in range(1, NY):
        j = lax.rem(y + k, NY)
        back.append(
            send(cslab.at[j], cbuf.at[y], c_s.at[k - 1], c_r.at[k - 1], tm_at(zh, j, x), head)
        )
    cbuf[y] = cslab[y]
    attend(6, 8)
    take(back)
    for g in range(blocks):
        at = slice(g * HD, (g + 1) * HD)
        per_block = HD // owned
        came = cbuf[g * per_block:(g + 1) * per_block].reshape(HD, WIDE).astype(F32)
        for i in range(NX):
            came = dxbuf[i, g:g + 1, :] * came
            stslab[i, at, :] = (sx[i, at, :] + came).astype(BF16)
    states = []
    for k in (2, 1, 3):
        j = lax.rem(x + k, NX)
        states.append(
            send(stslab.at[j], sbuf.at[x], st_s.at[k - 1], st_r.at[k - 1], tm_at(zh, y, j), head)
        )
    sbuf[x] = stslab[x]

    def divide(i, _):
        rows = pl.ds(pl.multiple_of(i * ROWS, ROWS), ROWS)
        first, second = res[0, rows, :], res[1, rows, :]
        total = pltpu.roll(jnp.where(low, second, first), HD, 1)
        res[0, rows, :] = jnp.where(low, first, second) / total
        return 0

    lax.fori_loop(0, TOKS // ROWS, divide, 0)
    take(states)
    for g in range(NB):
        state = sbuf[g // blocks, (g % blocks) * HD:(g % blocks + 1) * HD, :].astype(F32)
        sbd[g * WIDE:g * WIDE + HD, :] = jnp.where(low, state, 0.0).astype(BF16)
        sbd[g * WIDE + HD:(g + 1) * WIDE, :] = jnp.where(low, 0.0, state).astype(BF16)
    sent = []
    odd = lax.rem(z, 2)
    for n, zz in enumerate((lax.rem(z + 2, LINE), 3 - z, z + 1 - 2 * odd, z)):
        rows = pl.ds(pl.multiple_of(zz * ROWS, ROWS), ROWS)
        ids = bidb[rows, :]
        c32 = cc[rows, :].astype(F32)
        spread = jnp.concatenate(
            [jnp.where(ids == float(g), c32, 0.0).astype(BF16) for g in range(NB)], axis=1
        )
        readout = jnp.dot(spread, sbd[...], preferred_element_type=F32) * (1.0 / 512.0)
        mixed = (res[0, rows, :] + readout).astype(BF16).reshape(CORES, LOCAL, WIDE)
        mslab[pl.ds(zz * CORES, CORES)] = mixed
        for to in (core, 1 - core):
            if n == LINE - 1 and to is core:
                continue
            dest = zz * CORES + to
            k = 2 * n + (0 if to is core else 1)
            sent.append(
                send(mslab.at[dest], mbuf.at[head], m_s.at[k], m_r.at[k], tm, dest)
            )
    mbuf[head] = mslab[head]
    wo_copy.wait()
    take(sent)
    full = jnp.concatenate([mbuf[i] for i in range(HEADS_AXIS)], axis=1)
    out_ref[0] = jnp.dot(full, wo[...], preferred_element_type=F32).astype(BF16)

    for move in started:
        move.wait_send()


def body(frames_in, in_weight, out_weight, block_ids, block_lists, decays):
    vmem = pl.BlockSpec(memory_space=pltpu.VMEM)
    dma = pltpu.SemaphoreType.DMA
    scratch = [
        pltpu.VMEM((1, LOCAL, D), BF16),
        pltpu.VMEM((16, 5 * WIDE), BF16),
        pltpu.VMEM((HEADS_AXIS, LOCAL, D), BF16),
        pltpu.VMEM((NZ, NY, NX, 16, 5 * WIDE), BF16),
        pltpu.VMEM((D, D), BF16),
        pltpu.VMEM((TOKS, WIDE), F32),
        pltpu.VMEM((WIDE, WIDE), BF16),
        pltpu.VMEM((2, TOKS, WIDE), BF16),
        pltpu.VMEM((2, TOKS, WIDE), BF16),
        pltpu.VMEM((2, TOKS, WIDE), BF16),
        pltpu.VMEM((TOKS, WIDE), BF16),
        pltpu.VMEM((WIDE, NB * WIDE), F32),
        pltpu.VMEM((2, TOKS, WIDE), F32),
        pltpu.VMEM((NX, 256, WIDE), BF16),
        pltpu.VMEM((NX, 256, WIDE), BF16),
        pltpu.VMEM((NX, 256, WIDE), F32),
        pltpu.VMEM((NY, 32, WIDE), BF16),
        pltpu.VMEM((NZ, NY, 32, WIDE), BF16),
        pltpu.VMEM((NY, 32, WIDE), BF16),
        pltpu.VMEM((NY, 32, WIDE), BF16),
        pltpu.VMEM((NX, 256, WIDE), BF16),
        pltpu.VMEM((NX, 256, WIDE), BF16),
        pltpu.VMEM((NB * WIDE, WIDE), BF16),
        pltpu.VMEM((HEADS_AXIS, LOCAL, WIDE), BF16),
        pltpu.VMEM((HEADS_AXIS, LOCAL, WIDE), BF16),
        pltpu.VMEM((NX, 8, WIDE), F32),
        pltpu.VMEM((NX, 8, WIDE), F32),
        pltpu.VMEM((8, WIDE), F32),
        pltpu.VMEM((NZ, NY, 8, WIDE), F32),
    ]
    for shape in (
        (1,), (2, NX - 1), (2, 2, NY // 2), (2, LINE - 1, CHUNKS), (2 * LINE - 1, CHUNKS),
        (NX - 1,), (2, NY), (NX - 1,), (2, NY), (NY - 1,), (NX - 1,), (HEADS_AXIS,),
    ):
        scratch += [dma(shape), dma(shape)]
    scratch.append(dma((3,)))
    hbm = pl.BlockSpec(memory_space=pl.ANY)
    return pl.pallas_call(
        kernel,
        out_shape=jax.ShapeDtypeStruct((1, LOCAL, D), BF16),
        in_specs=[hbm, hbm, hbm, vmem, vmem, vmem],
        out_specs=vmem,
        scratch_shapes=scratch,
        compiler_params=pltpu.CompilerParams(
            collective_id=0, has_side_effects=True, vmem_limit_bytes=56 * 1024 * 1024
        ),
        name="layer",
    )(frames_in, in_weight, out_weight, block_ids.reshape(1, TOKS), block_lists.T, decays)


def solution(mesh):
    return jax.shard_map(
        body,
        mesh=mesh,
        in_specs=(P("tm", "head", None), P("tm", "head"), P(), P(), P(), P("tm", "head", None)),
        out_specs=P("tm", "head", None),
        check_vma=False,
    )
```

time: 88.9 us -> 76.2 us (0.86)
  Pallas kernels: 85.7 us -> 74.3 us
  local copies, waits for them, and re-layouts: 3.02 us -> 1.67 us
    pallas_call x1, Pallas kernels: 85.7 us -> 74.3 us  [body(): pl.pallas_call(kernel, out_shape=jax.ShapeDtypeStruct((1, LOCAL, D), BF16...]
    unnamed x2 -> x1, local copies, waits for them, and re-layouts: 3.02 us -> 1.67 us
where the time goes in v2:
time: 76.2 us; the launch traced here: 76 us
  Pallas kernels  74.3 us (98%)
  local copies, waits for them, and re-layouts  1.67 us (2%)
    pallas_call x1, Pallas kernels, body(): pl.pallas_call(kernel, out_shape=jax.ShapeDtypeStruct((1, LOCAL, D), BF16...  74.3 us
    unnamed x1, local copies, waits for them, and re-layouts  1.67 us

profile of v2, /device:TPU:1, one launch (start us, length us, event | category | flops | bytes accessed | tf_op | source)
XLA Modules:
  0.0 76.0 jit_solution(3047843436927470844)
XLA Ops:
  0.0 74.3 %layer.1 = bf16[1,128,1024]{2,1,0:T(8,128)(2,1)} custom-call(bf16[1,128,1024]{2,1,0:T(8,128)(2,1)} %x_hbm.1, bf16[16,640]{1,0:T(8,128)(2,1)} %w_hbm.1, bf16[1024,1024]{1,0:T(8,128)(2,1)} %wo_hbm.1, s32[1,1024]{1,0:T(1,128)} %bitcast.2, s32[4,16]{1,0:T(4,128)} %bitcast.3, f32[1,2,16]{2,1,0:T(2,128)} %dec_ref.1), custom_call_target="tpu_custom_call" | custom-call | tf_op jit(solution)/shard_map/layer/pallas_call | solution.py:474
  74.3 1.7 %copy.8 = bf16[1,128,1024]{2,1,0:T(8,128)(2,1)} copy(bf16[1,128,1024]{2,1,0:T(8,128)(2,1)} %layer.1) | data formatting | bytes 524288

commit v3 on v2

--- a/solution.py
+++ b/solution.py
@@ -42,7 +42,7 @@
 
 def kernel(
     x_hbm, w_hbm, wo_hbm, bid_ref, lists_ref, dec_ref, out_ref,
-    xin, win, xbuf, wbuf, wo, bidb, fmat, qa, ka, va, cc, acc, res,
+    xin, win, xbuf, wvb, wqkc, wo, bidb, fmat, qa, ka, va, cc, acc, res,
     sslab, ubuf, sx, tslab, tbuf, cslab, cbuf, stslab, sbuf, sbd, mslab, mbuf,
     dout, dxbuf, pdout, pdbuf,
     wz_s, wz_r, wx_s, wx_r, wy_s, wy_r, xg_s, xg_r, sib_s, sib_r,
@@ -94,6 +94,107 @@
 
     lane = lax.broadcasted_iota(jnp.int32, (1, WIDE), 1)
     low = lane < HD
+
+    loads[0].wait()
+    raw = [win[:, i * WIDE:(i + 1) * WIDE].astype(F32) for i in range(5)]
+    swap = functools.partial(pltpu.roll, shift=HD, axis=1)
+    ordered = [
+        jnp.where(low, raw[1], raw[3]),
+        swap(jnp.where(low, raw[4], raw[1])),
+        jnp.where(low, raw[0], raw[2]),
+        swap(jnp.where(low, raw[3], raw[0])),
+        jnp.where(low, raw[2], raw[4]),
+    ]
+    for i in range(5):
+        buf, col = (wvb, i) if i < 2 else (wqkc, i - 2)
+        buf[zh, y, x, :, col * WIDE:(col + 1) * WIDE] = ordered[i].astype(BF16)
+
+    per = LOCAL // CHUNKS
+
+    def part(source, k):
+        return xbuf.at[source * CORES + core, pl.ds(k * per, per)]
+
+    def is_source(zz):
+        return (zz >= 0) & (zz < LINE)
+
+    line, sib = {}, {}
+
+    def send_line(way, s, k):
+        source, to = (z - (s - 1), z + 1) if way == 0 else (z + (s - 1), z - 1)
+        come = is_source(z - s if way == 0 else z + s)
+        ref = part(source, k)
+        line[way, s, k] = send(
+            ref, ref, xg_s.at[way, s - 1, k], xg_r.at[way, s - 1, k], tm, to * CORES + core,
+            is_source(source) & is_source(to), come,
+        )
+
+    def send_sib(n, source, k, go=None, come=None):
+        ref = part(source, k)
+        sib[n, k] = send(
+            ref, ref, sib_s.at[n, k], sib_r.at[n, k], tm, z * CORES + 1 - core, go, come
+        )
+
+    def take_line(s, k):
+        for way in range(2):
+            move = line[way, s, k]
+            move.wait_recv()
+            if s < LINE - 1:
+                send_line(way, s + 1, k)
+            send_sib(2 * s - 1 + way, z - s if way == 0 else z + s, k, move.come, move.come)
+
+    parts = (wvb, wqkc)
+
+    def send_z(c):
+        ref = parts[c].at[zh, y, x]
+        return [send(ref, ref, wz_s.at[c], wz_r.at[c], tm_at(1 - zh, y, x), head)]
+
+    def send_x(c, side):
+        ref = parts[c].at[zh if side == 0 else 1 - zh, y, x]
+        return [
+            send(ref, ref, wx_s.at[c, side, k - 1], wx_r.at[c, side, k - 1],
+                 tm_at(zh, y, lax.rem(x + k, NX)), head)
+            for k in range(1, NX)
+        ]
+
+    def take(moves):
+        for move in moves:
+            move.wait_recv()
+
+    rings = {}
+
+    def send_ring(c, side, s):
+        half = zh if side == 0 else 1 - zh
+        rings[c, side, s] = []
+        for way in range(2) if s < NY // 2 else (side,):
+            held = lax.rem(y - (s - 1) + NY, NY) if way == 0 else lax.rem(y + (s - 1), NY)
+            to = lax.rem(y + (1 if way == 0 else NY - 1), NY)
+            ref = parts[c].at[half, held]
+            rings[c, side, s].append(
+                send(ref, ref, wy_s.at[c, side, way, s - 1], wy_r.at[c, side, way, s - 1],
+                     tm_at(zh, to, x), head)
+            )
+
+    def forward(c, side, s):
+        take(rings[c, side, s])
+        if s < NY // 2:
+            send_ring(c, side, s + 1)
+
+    pl.semaphore_wait(barrier, expected)
+    far = send_z(0)
+    own = send_x(0, 0)
+    loads[1].wait()
+    wide = xin[0].astype(F32)
+    xbuf[head] = (
+        wide * lax.rsqrt(jnp.mean(wide * wide, axis=-1, keepdims=True) + EPS)
+    ).astype(BF16)
+    for k in range(CHUNKS):
+        for way in range(2):
+            send_line(way, 1, k)
+        send_sib(0, z, k)
+    far_late = send_z(1)
+    own_late = send_x(1, 0)
+    take(own)
+    send_ring(0, 0, 1)
 
     dec = dec_ref[0]
     gi = lax.broadcasted_iota(jnp.int32, (NB, NB), 0)
@@ -107,98 +208,16 @@
         dout[j, 0:4, :] = drow[4 * j:4 * j + 4, :]
     dxbuf[x] = dout[x]
 
-    loads[0].wait()
-    raw = [win[:, i * WIDE:(i + 1) * WIDE].astype(F32) for i in range(5)]
-    swap = functools.partial(pltpu.roll, shift=HD, axis=1)
-    ordered = [
-        jnp.where(low, raw[1], raw[3]),
-        swap(jnp.where(low, raw[4], raw[1])),
-        jnp.where(low, raw[0], raw[2]),
-        swap(jnp.where(low, raw[3], raw[0])),
-        jnp.where(low, raw[2], raw[4]),
-    ]
-    mine = wbuf.at[zh, y, x]
-    for i in range(5):
-        mine[:, i * WIDE:(i + 1) * WIDE] = ordered[i].astype(BF16)
-
-    loads[1].wait()
-    wide = xin[0].astype(F32)
-    xbuf[head] = (
-        wide * lax.rsqrt(jnp.mean(wide * wide, axis=-1, keepdims=True) + EPS)
-    ).astype(BF16)
-    per = LOCAL // CHUNKS
-
-    def part(source, k):
-        return xbuf.at[source * CORES + core, pl.ds(k * per, per)]
-
-    def is_source(zz):
-        return (zz >= 0) & (zz < LINE)
-
-    line, sib = {}, {}
-
-    def send_line(way, s, k):
-        source, to = (z - (s - 1), z + 1) if way == 0 else (z + (s - 1), z - 1)
-        come = is_source(z - s if way == 0 else z + s)
-        ref = part(source, k)
-        line[way, s, k] = send(
-            ref, ref, xg_s.at[way, s - 1, k], xg_r.at[way, s - 1, k], tm, to * CORES + core,
-            is_source(source) & is_source(to), come,
-        )
-
-    def send_sib(n, source, k, go=None, come=None):
-        ref = part(source, k)
-        sib[n, k] = send(
-            ref, ref, sib_s.at[n, k], sib_r.at[n, k], tm, z * CORES + 1 - core, go, come
-        )
-
-    def take_line(s, k):
-        for way in range(2):
-            move = line[way, s, k]
-            move.wait_recv()
-            if s < LINE - 1:
-                send_line(way, s + 1, k)
-            send_sib(2 * s - 1 + way, z - s if way == 0 else z + s, k, move.come, move.come)
-
-    def send_x(side):
-        ref = wbuf.at[zh if side == 0 else 1 - zh, y, x]
-        return [
-            send(ref, ref, wx_s.at[side, k - 1], wx_r.at[side, k - 1],
-                 tm_at(zh, y, lax.rem(x + k, NX)), head)
-            for k in range(1, NX)
-        ]
-
-    def send_ring(side, s):
-        half = zh if side == 0 else 1 - zh
-        moves = []
-        for way in range(2) if s < NY // 2 else (side,):
-            held = lax.rem(y - (s - 1) + NY, NY) if way == 0 else lax.rem(y + (s - 1), NY)
-            to = lax.rem(y + (1 if way == 0 else NY - 1), NY)
-            ref = wbuf.at[half, held]
-            moves.append(
-                send(ref, ref, wy_s.at[side, way, s - 1], wy_r.at[side, way, s - 1],
-                     tm_at(zh, to, x), head)
-            )
-        return moves
-
-    def take(moves):
-        for move in moves:
-            move.wait_recv()
-
-    pl.semaphore_wait(barrier, expected)
-    wz = send(mine, mine, wz_s.at[0], wz_r.at[0], tm_at(1 - zh, y, x), head)
-    own = send_x(0)
-    for k in range(CHUNKS):
-        for way in range(2):
-            send_line(way, 1, k)
-        send_sib(0, z, k)
     dx = []
     for k in range(1, NX):
         j = lax.rem(x + k, NX)
         dx.append(
             send(dout.at[j], dxbuf.at[x], dx_s.at[k - 1], dx_r.at[k - 1], tm_at(zh, y, j), head)
         )
-    take(own)
-    rings = {(0, 1): send_ring(0, 1)}
+    take_line(1, 0)
+    take(far)
+    other = send_x(0, 1)
+    forward(0, 0, 1)
 
     ids = jnp.broadcast_to(bid_ref[...].astype(F32), (WIDE, TOKS))
     for i in range(TOKS // WIDE):
@@ -211,61 +230,38 @@
     for k in range(lists_ref.shape[0]):
         adjacent = adjacent | (lists_ref[k:k + 1, :] == key_block)
     fmat[:, 0:NB] = jnp.where(adjacent, 0.0, FAR).astype(BF16)
-    acc[...] = jnp.zeros_like(acc)
-
-    def forward(side, s):
-        take(rings[side, s])
-        if s < NY // 2:
-            rings[side, s + 1] = send_ring(side, s + 1)
-
-    take_line(1, 0)
-    wz.wait_recv()
-    other = send_x(1)
-    forward(0, 1)
+
     take_line(1, 1)
     take(other)
-    rings[1, 1] = send_ring(1, 1)
-    forward(0, 2)
+    send_ring(0, 1, 1)
+    forward(0, 0, 2)
+    take(far_late)
+    other_late = send_x(1, 1)
     take_line(2, 0)
-    forward(1, 1)
-    forward(0, 3)
+    forward(0, 1, 1)
+    forward(0, 0, 3)
+    take(own_late)
+    send_ring(1, 0, 1)
+    forward(0, 1, 2)
+    take_line(2, 1)
+    forward(0, 0, 4)
+    forward(0, 1, 3)
+    take(other_late)
+    send_ring(1, 1, 1)
     take(dx)
     prod = dxbuf[0]
     for i in range(1, NX):
         prod = prod * dxbuf[i]
     pdout[...] = prod
     pdbuf[zh, y] = prod
-    take_line(2, 1)
-    forward(1, 2)
+    forward(1, 0, 1)
+    forward(0, 1, 4)
     take_line(3, 0)
-    forward(0, 4)
-    forward(1, 3)
-    take_line(3, 1)
-    for move in sib.values():
-        move.wait_recv()
-    forward(1, 4)
-
-    first_half, second_half = zh == 0, zh == 1
-
-    def to_group(src_of, dst, ssem, rsem):
-        moves = []
-        for k in range(NY):
-            j = lax.rem(y + k, NY)
-            moves.append(
-                send(src_of(j), dst.at[0, y], ssem.at[1, k], rsem.at[1, k], tm_at(1, j, x), head,
-                     first_half, second_half)
-            )
-        for k in range(1, NY):
-            j = lax.rem(y + k, NY)
-            moves.append(
-                send(src_of(j), dst.at[zh, y], ssem.at[0, k], rsem.at[0, k], tm_at(zh, j, x), head)
-            )
-        return moves
-
-    def project_vb(i, _):
-        rows = pl.ds(pl.multiple_of(i * ROWS, ROWS), ROWS)
-        tokens = xbuf[pl.ds(i * (ROWS // LOCAL), ROWS // LOCAL)].reshape(ROWS, D)
-        weights = wbuf[:, :, :, :, 0:2 * WIDE].reshape(D, 2 * WIDE)
+
+    def project_vb(zz, first):
+        rows = pl.ds(pl.multiple_of(zz * ROWS, ROWS), ROWS)
+        tokens = xbuf[pl.ds(zz * CORES, CORES)].reshape(ROWS, D)
+        weights = wvb[...].reshape(D, 2 * WIDE)
         p = jnp.dot(tokens, weights, preferred_element_type=F32).astype(BF16).astype(F32)
         v, b = p[:, 0:WIDE], p[:, WIDE:2 * WIDE]
         ids = bidb[rows, :]
@@ -277,10 +273,37 @@
                 [jnp.where(ids == float(g + n), v, 0.0).astype(BF16) for n in range(4)], axis=1
             )
             at = slice(g * WIDE, (g + 4) * WIDE)
-            acc[:, at] += jnp.dot(bt, masked, preferred_element_type=F32)
-        return 0
-
-    lax.fori_loop(0, TOKS // ROWS, project_vb, 0)
+            term = jnp.dot(bt, masked, preferred_element_type=F32)
+            acc[:, at] = term if first else acc[:, at] + term
+
+    odd = lax.rem(z, 2)
+    nearest = (z, z + 1 - 2 * odd, lax.rem(z + 2, LINE), 3 - z)
+    for n in range(LINE):
+        if n == LINE - 1:
+            forward(1, 1, 1)
+            take_line(3, 1)
+        for way in range(2) if n else (0,):
+            for k in range(CHUNKS):
+                sib[2 * n - 1 + way if n else 0, k].wait_recv()
+        project_vb(nearest[n], n == 0)
+
+    first_half, second_half = zh == 0, zh == 1
+
+    def to_group(src_of, dst, ssem, rsem):
+        moves = []
+        for k in range(NY):
+            j = lax.rem(y + k, NY)
+            moves.append(
+                send(src_of(j), dst.at[0, y], ssem.at[1, k], rsem.at[1, k], tm_at(1, j, x), head,
+                     first_half, second_half)
+            )
+        for k in range(1, NY):
+            j = lax.rem(y + k, NY)
+            moves.append(
+                send(src_of(j), dst.at[zh, y], ssem.at[0, k], rsem.at[0, k], tm_at(zh, j, x), head)
+            )
+        return moves
+
     for g in range(NB):
         at = slice(g * WIDE, (g + 1) * WIDE)
         both = jnp.where(low, acc[0:HD, at], acc[HD:WIDE, at])
@@ -305,7 +328,7 @@
     def project_qkc(i, _):
         rows = pl.ds(pl.multiple_of(i * ROWS, ROWS), ROWS)
         tokens = xbuf[pl.ds(i * (ROWS // LOCAL), ROWS // LOCAL)].reshape(ROWS, D)
-        weights = wbuf[:, :, :, :, 2 * WIDE:].reshape(D, 3 * WIDE)
+        weights = wqkc[...].reshape(D, 3 * WIDE)
         p = jnp.dot(tokens, weights, preferred_element_type=F32).astype(BF16)
         q, k, c = (p[:, j * WIDE:(j + 1) * WIDE] for j in range(3))
         hot = jnp.where(bidb[rows, :] == wrapped_f, 1.0, 0.0)
@@ -321,8 +344,6 @@
         cc[rows, :] = c
         return 0
 
-    lax.fori_loop(0, TOKS // ROWS, project_qkc, 0)
-
     def attend(first, last):
         def one(n, _):
             h, i = lax.div(n, TOKS // ROWS), lax.rem(n, TOKS // ROWS)
@@ -337,7 +358,9 @@
 
         lax.fori_loop(first, last, one, 0)
 
-    attend(0, 2)
+    forward(1, 0, 2)
+    forward(1, 1, 2)
+    forward(1, 0, 3)
     take(up)
     blocks, owned = NB // NX, 32
     for g in range(blocks):
@@ -352,7 +375,11 @@
             tslab[g * (HD // owned) + n] = piece
     tot = to_group(lambda j: tslab.at[j], tbuf, t_s, t_r)
     tbuf[zh, y] = tslab[y]
-    attend(2, 6)
+    forward(1, 1, 3)
+    take(rings[1, 0, NY // 2])
+    take(rings[1, 1, NY // 2])
+    lax.fori_loop(0, TOKS // ROWS, project_qkc, 0)
+    attend(0, 3)
     take(pd)
     take(tot)
     own_block = pl.ds(lax.div(y, HD // owned), 1)
@@ -370,7 +397,7 @@
             send(cslab.at[j], cbuf.at[y], c_s.at[k - 1], c_r.at[k - 1], tm_at(zh, j, x), head)
         )
     cbuf[y] = cslab[y]
-    attend(6, 8)
+    attend(3, 8)
     take(back)
     for g in range(blocks):
         at = slice(g * HD, (g + 1) * HD)
@@ -401,8 +428,7 @@
         sbd[g * WIDE:g * WIDE + HD, :] = jnp.where(low, state, 0.0).astype(BF16)
         sbd[g * WIDE + HD:(g + 1) * WIDE, :] = jnp.where(low, 0.0, state).astype(BF16)
     sent = []
-    odd = lax.rem(z, 2)
-    for n, zz in enumerate((lax.rem(z + 2, LINE), 3 - z, z + 1 - 2 * odd, z)):
+    for n, zz in enumerate((nearest[2], nearest[3], nearest[1], nearest[0])):
         rows = pl.ds(pl.multiple_of(zz * ROWS, ROWS), ROWS)
         ids = bidb[rows, :]
         c32 = cc[rows, :].astype(F32)
@@ -437,7 +463,8 @@
         pltpu.VMEM((1, LOCAL, D), BF16),
         pltpu.VMEM((16, 5 * WIDE), BF16),
         pltpu.VMEM((HEADS_AXIS, LOCAL, D), BF16),
-        pltpu.VMEM((NZ, NY, NX, 16, 5 * WIDE), BF16),
+        pltpu.VMEM((NZ, NY, NX, 16, 2 * WIDE), BF16),
+        pltpu.VMEM((NZ, NY, NX, 16, 3 * WIDE), BF16),
         pltpu.VMEM((D, D), BF16),
         pltpu.VMEM((TOKS, WIDE), F32),
         pltpu.VMEM((WIDE, WIDE), BF16),
@@ -465,7 +492,7 @@
         pltpu.VMEM((NZ, NY, 8, WIDE), F32),
     ]
     for shape in (
-        (1,), (2, NX - 1), (2, 2, NY // 2), (2, LINE - 1, CHUNKS), (2 * LINE - 1, CHUNKS),
+        (2,), (2, 2, NX - 1), (2, 2, 2, NY // 2), (2, LINE - 1, CHUNKS), (2 * LINE - 1, CHUNKS),
         (NX - 1,), (2, NY), (NX - 1,), (2, NY), (NY - 1,), (NX - 1,), (HEADS_AXIS,),
     ):
         scratch += [dma(shape), dma(shape)]

time: 76.2 us -> 78.1 us (1.025)
  Pallas kernels: 74.3 us -> 76.2 us
    pallas_call x1, Pallas kernels: 74.3 us -> 76.2 us  [body(): pl.pallas_call(kernel, out_shape=jax.ShapeDtypeStruct((1, LOCAL, D), BF16...]
where the time goes in v3:
time: 78.1 us; the launch traced here: 77.9 us
  Pallas kernels  76.2 us (98%)
  local copies, waits for them, and re-layouts  1.67 us (2%)
    pallas_call x1, Pallas kernels, body(): pl.pallas_call(kernel, out_shape=jax.ShapeDtypeStruct((1, LOCAL, D), BF16...  76.2 us
    unnamed x1, local copies, waits for them, and re-layouts  1.67 us

profile of v3, /device:TPU:1, one launch (start us, length us, event | category | flops | bytes accessed | tf_op | source)
XLA Modules:
  0.0 77.9 jit_solution(4231073624046307927)
XLA Ops:
  0.0 76.2 %layer.1 = bf16[1,128,1024]{2,1,0:T(8,128)(2,1)} custom-call(bf16[1,128,1024]{2,1,0:T(8,128)(2,1)} %x_hbm.1, bf16[16,640]{1,0:T(8,128)(2,1)} %w_hbm.1, bf16[1024,1024]{1,0:T(8,128)(2,1)} %wo_hbm.1, s32[1,1024]{1,0:T(1,128)} %bitcast.2, s32[4,16]{1,0:T(4,128)} %bitcast.3, f32[1,2,16]{2,1,0:T(2,128)} %dec_ref.1), custom_call_target="tpu_custom_call" | custom-call | tf_op jit(solution)/shard_map/layer/pallas_call | solution.py:501
  76.2 1.7 %copy.8 = bf16[1,128,1024]{2,1,0:T(8,128)(2,1)} copy(bf16[1,128,1024]{2,1,0:T(8,128)(2,1)} %layer.1) | data formatting | bytes 524288

commit v4 on v3

--- a/solution.py
+++ b/solution.py
@@ -17,7 +17,8 @@
 NG = NY * NZ
 LINE, CORES = 4, 2
 HEADS_AXIS = LINE * CORES
-CHUNKS = 2
+CHUNKS = 4
+PAIRS = 2
 ROWS = 256
 EPS = 1e-6
 FAR = -256.0
@@ -45,7 +46,7 @@
     xin, win, xbuf, wvb, wqkc, wo, bidb, fmat, qa, ka, va, cc, acc, res,
     sslab, ubuf, sx, tslab, tbuf, cslab, cbuf, stslab, sbuf, sbd, mslab, mbuf,
     dout, dxbuf, pdout, pdbuf,
-    wz_s, wz_r, wx_s, wx_r, wy_s, wy_r, xg_s, xg_r, sib_s, sib_r,
+    wz_s, wz_r, wx_s, wx_r, wd_s, wd_r, wy_s, wy_r, xg_s, xg_r, sib_s, sib_r,
     dx_s, dx_r, pd_s, pd_r, u_s, u_r, t_s, t_r, c_s, c_r, st_s, st_r, m_s, m_r, in_sem,
 ):
     tm, head = lax.axis_index("tm"), lax.axis_index("head")
@@ -65,12 +66,12 @@
     greet(tm_at(zh, y, lax.rem(x + 2, NX)), head)
     for k in (1, NX - 1):
         greet(tm_at(zh, y, lax.rem(x + k, NX)), head)
-    for k in (1, NY - 1):
+    for k in (4, 3, 5, 2, 6, 1, 7):
         greet(tm_at(zh, lax.rem(y + k, NY), x), head)
     pl.when(z > 0)(lambda: greet(tm, head - CORES))
     pl.when(z < LINE - 1)(lambda: greet(tm, head + CORES))
     greet(tm, z * CORES + 1 - core)
-    expected = 7 + (z > 0).astype(jnp.int32) + (z < LINE - 1).astype(jnp.int32)
+    expected = 12 + (z > 0).astype(jnp.int32) + (z < LINE - 1).astype(jnp.int32)
 
     loads = [
         pltpu.make_async_copy(src, dst, in_sem.at[i])
@@ -109,10 +110,9 @@
         buf, col = (wvb, i) if i < 2 else (wqkc, i - 2)
         buf[zh, y, x, :, col * WIDE:(col + 1) * WIDE] = ordered[i].astype(BF16)
 
-    per = LOCAL // CHUNKS
-
-    def part(source, k):
-        return xbuf.at[source * CORES + core, pl.ds(k * per, per)]
+
+    def part(source, k, size=LOCAL // CHUNKS):
+        return xbuf.at[source * CORES + core, pl.ds(k * size, size)]
 
     def is_source(zz):
         return (zz >= 0) & (zz < LINE)
@@ -129,7 +129,7 @@
         )
 
     def send_sib(n, source, k, go=None, come=None):
-        ref = part(source, k)
+        ref = part(source, k, LOCAL // PAIRS)
         sib[n, k] = send(
             ref, ref, sib_s.at[n, k], sib_r.at[n, k], tm, z * CORES + 1 - core, go, come
         )
@@ -140,7 +140,11 @@
             move.wait_recv()
             if s < LINE - 1:
                 send_line(way, s + 1, k)
-            send_sib(2 * s - 1 + way, z - s if way == 0 else z + s, k, move.come, move.come)
+            if k % (CHUNKS // PAIRS) == CHUNKS // PAIRS - 1:
+                send_sib(
+                    2 * s - 1 + way, z - s if way == 0 else z + s, k // (CHUNKS // PAIRS),
+                    move.come, move.come,
+                )
 
     parts = (wvb, wqkc)
 
@@ -162,22 +166,30 @@
 
     rings = {}
 
-    def send_ring(c, side, s):
+    def send_y(side):
+        ref = wvb.at[zh if side == 0 else 1 - zh, y]
+        return [
+            send(ref, ref, wd_s.at[side, k - 1], wd_r.at[side, k - 1],
+                 tm_at(zh, lax.rem(y + k, NY), x), head)
+            for k in (4, 3, 5, 2, 6, 1, 7)
+        ]
+
+    def send_ring(side, s):
         half = zh if side == 0 else 1 - zh
-        rings[c, side, s] = []
+        rings[side, s] = []
         for way in range(2) if s < NY // 2 else (side,):
             held = lax.rem(y - (s - 1) + NY, NY) if way == 0 else lax.rem(y + (s - 1), NY)
             to = lax.rem(y + (1 if way == 0 else NY - 1), NY)
-            ref = parts[c].at[half, held]
-            rings[c, side, s].append(
-                send(ref, ref, wy_s.at[c, side, way, s - 1], wy_r.at[c, side, way, s - 1],
+            ref = wqkc.at[half, held]
+            rings[side, s].append(
+                send(ref, ref, wy_s.at[side, way, s - 1], wy_r.at[side, way, s - 1],
                      tm_at(zh, to, x), head)
             )
 
-    def forward(c, side, s):
-        take(rings[c, side, s])
+    def forward(side, s):
+        take(rings[side, s])
         if s < NY // 2:
-            send_ring(c, side, s + 1)
+            send_ring(side, s + 1)
 
     pl.semaphore_wait(barrier, expected)
     far = send_z(0)
@@ -190,11 +202,12 @@
     for k in range(CHUNKS):
         for way in range(2):
             send_line(way, 1, k)
+    for k in range(PAIRS):
         send_sib(0, z, k)
     far_late = send_z(1)
     own_late = send_x(1, 0)
     take(own)
-    send_ring(0, 0, 1)
+    direct = send_y(0)
 
     dec = dec_ref[0]
     gi = lax.broadcasted_iota(jnp.int32, (NB, NB), 0)
@@ -217,7 +230,7 @@
     take_line(1, 0)
     take(far)
     other = send_x(0, 1)
-    forward(0, 0, 1)
+    take_line(1, 1)
 
     ids = jnp.broadcast_to(bid_ref[...].astype(F32), (WIDE, TOKS))
     for i in range(TOKS // WIDE):
@@ -231,32 +244,29 @@
         adjacent = adjacent | (lists_ref[k:k + 1, :] == key_block)
     fmat[:, 0:NB] = jnp.where(adjacent, 0.0, FAR).astype(BF16)
 
-    take_line(1, 1)
+    take_line(1, 2)
     take(other)
-    send_ring(0, 1, 1)
-    forward(0, 0, 2)
+    direct += send_y(1)
+    take_line(1, 3)
     take(far_late)
     other_late = send_x(1, 1)
     take_line(2, 0)
-    forward(0, 1, 1)
-    forward(0, 0, 3)
+    take_line(2, 1)
     take(own_late)
-    send_ring(1, 0, 1)
-    forward(0, 1, 2)
-    take_line(2, 1)
-    forward(0, 0, 4)
-    forward(0, 1, 3)
-    take(other_late)
-    send_ring(1, 1, 1)
+    send_ring(0, 1)
+    take_line(2, 2)
     take(dx)
     prod = dxbuf[0]
     for i in range(1, NX):
         prod = prod * dxbuf[i]
     pdout[...] = prod
     pdbuf[zh, y] = prod
-    forward(1, 0, 1)
-    forward(0, 1, 4)
+    take_line(2, 3)
+    take(other_late)
+    send_ring(1, 1)
     take_line(3, 0)
+    take_line(3, 1)
+    take(direct)
 
     def project_vb(zz, first):
         rows = pl.ds(pl.multiple_of(zz * ROWS, ROWS), ROWS)
@@ -280,10 +290,10 @@
     nearest = (z, z + 1 - 2 * odd, lax.rem(z + 2, LINE), 3 - z)
     for n in range(LINE):
         if n == LINE - 1:
-            forward(1, 1, 1)
-            take_line(3, 1)
+            take_line(3, 2)
+            take_line(3, 3)
         for way in range(2) if n else (0,):
-            for k in range(CHUNKS):
+            for k in range(PAIRS):
                 sib[2 * n - 1 + way if n else 0, k].wait_recv()
         project_vb(nearest[n], n == 0)
 
@@ -315,6 +325,8 @@
             send(sslab.at[j], ubuf.at[x], u_s.at[k - 1], u_r.at[k - 1], tm_at(zh, y, j), head)
         )
     ubuf[x] = sslab[x]
+    forward(0, 1)
+    forward(1, 1)
     pd = to_group(lambda j: pdout, pdbuf, pd_s, pd_r)
 
     def normed_heads(values):
@@ -325,42 +337,31 @@
         ]
         return (values * lax.rsqrt(jnp.where(low, means[0], means[1]) + EPS)).astype(BF16).astype(F32)
 
-    def project_qkc(i, _):
-        rows = pl.ds(pl.multiple_of(i * ROWS, ROWS), ROWS)
-        tokens = xbuf[pl.ds(i * (ROWS // LOCAL), ROWS // LOCAL)].reshape(ROWS, D)
+    def project_qkc():
+        tokens = xbuf[...].reshape(TOKS, D)
         weights = wqkc[...].reshape(D, 3 * WIDE)
         p = jnp.dot(tokens, weights, preferred_element_type=F32).astype(BF16)
         q, k, c = (p[:, j * WIDE:(j + 1) * WIDE] for j in range(3))
-        hot = jnp.where(bidb[rows, :] == wrapped_f, 1.0, 0.0)
+        hot = jnp.where(bidb[...] == wrapped_f, 1.0, 0.0)
         banned = lax.dot_general(
             hot.astype(BF16), fmat[...], (((1,), (1,)), ((), ())), preferred_element_type=F32
         )
         qn = normed_heads(q.astype(F32)) * 0.125
         kn = normed_heads(k.astype(F32))
-        qa[0, rows, :] = jnp.where(low, qn, banned).astype(BF16)
-        qa[1, rows, :] = jnp.where(low, banned, qn).astype(BF16)
-        ka[0, rows, :] = jnp.where(low, kn, hot).astype(BF16)
-        ka[1, rows, :] = jnp.where(low, hot, kn).astype(BF16)
-        cc[rows, :] = c
-        return 0
-
-    def attend(first, last):
-        def one(n, _):
-            h, i = lax.div(n, TOKS // ROWS), lax.rem(n, TOKS // ROWS)
-            rows = pl.ds(pl.multiple_of(i * ROWS, ROWS), ROWS)
-            score = lax.dot_general(
-                qa[h, rows, :], ka[h], (((1,), (1,)), ((), ())), preferred_element_type=F32
-            )
-            res[h, rows, :] = jnp.dot(
-                jnp.exp(score).astype(BF16), va[h], preferred_element_type=F32
-            )
-            return 0
-
-        lax.fori_loop(first, last, one, 0)
-
-    forward(1, 0, 2)
-    forward(1, 1, 2)
-    forward(1, 0, 3)
+        qa[0, :, :] = jnp.where(low, qn, banned).astype(BF16)
+        qa[1, :, :] = jnp.where(low, banned, qn).astype(BF16)
+        ka[0, :, :] = jnp.where(low, kn, hot).astype(BF16)
+        ka[1, :, :] = jnp.where(low, hot, kn).astype(BF16)
+        cc[...] = c
+
+    def attend(h):
+        score = lax.dot_general(
+            qa[h], ka[h], (((1,), (1,)), ((), ())), preferred_element_type=F32
+        )
+        res[h] = jnp.dot(jnp.exp(score).astype(BF16), va[h], preferred_element_type=F32)
+
+    forward(0, 2)
+    forward(1, 2)
     take(up)
     blocks, owned = NB // NX, 32
     for g in range(blocks):
@@ -375,11 +376,12 @@
             tslab[g * (HD // owned) + n] = piece
     tot = to_group(lambda j: tslab.at[j], tbuf, t_s, t_r)
     tbuf[zh, y] = tslab[y]
-    forward(1, 1, 3)
-    take(rings[1, 0, NY // 2])
-    take(rings[1, 1, NY // 2])
-    lax.fori_loop(0, TOKS // ROWS, project_qkc, 0)
-    attend(0, 3)
+    forward(0, 3)
+    forward(1, 3)
+    take(rings[0, NY // 2])
+    take(rings[1, NY // 2])
+    project_qkc()
+    attend(0)
     take(pd)
     take(tot)
     own_block = pl.ds(lax.div(y, HD // owned), 1)
@@ -397,7 +399,7 @@
             send(cslab.at[j], cbuf.at[y], c_s.at[k - 1], c_r.at[k - 1], tm_at(zh, j, x), head)
         )
     cbuf[y] = cslab[y]
-    attend(3, 8)
+    attend(1)
     take(back)
     for g in range(blocks):
         at = slice(g * HD, (g + 1) * HD)
@@ -448,11 +450,14 @@
             )
     mbuf[head] = mslab[head]
     wo_copy.wait()
+    for move in started:
+        if move not in sent:
+            move.wait_send()
     take(sent)
     full = jnp.concatenate([mbuf[i] for i in range(HEADS_AXIS)], axis=1)
     out_ref[0] = jnp.dot(full, wo[...], preferred_element_type=F32).astype(BF16)
 
-    for move in started:
+    for move in sent:
         move.wait_send()
 
 
@@ -492,7 +497,8 @@
         pltpu.VMEM((NZ, NY, 8, WIDE), F32),
     ]
     for shape in (
-        (2,), (2, 2, NX - 1), (2, 2, 2, NY // 2), (2, LINE - 1, CHUNKS), (2 * LINE - 1, CHUNKS),
+        (2,), (2, 2, NX - 1), (2, NY - 1), (2, 2, NY // 2), (2, LINE - 1, CHUNKS),
+        (2 * LINE - 1, PAIRS),
         (NX - 1,), (2, NY), (NX - 1,), (2, NY), (NY - 1,), (NX - 1,), (HEADS_AXIS,),
     ):
         scratch += [dma(shape), dma(shape)]

time: 78.1 us -> 75 us (0.960)
  Pallas kernels: 76.2 us -> 73.2 us
    pallas_call x1, Pallas kernels: 76.2 us -> 73.2 us  [body(): pl.pallas_call(kernel, out_shape=jax.ShapeDtypeStruct((1, LOCAL, D), BF16...]
where the time goes in v4:
time: 75 us; the launch traced here: 74.9 us
  Pallas kernels  73.2 us (98%)
  local copies, waits for them, and re-layouts  1.67 us (2%)
    pallas_call x1, Pallas kernels, body(): pl.pallas_call(kernel, out_shape=jax.ShapeDtypeStruct((1, LOCAL, D), BF16...  73.2 us
    unnamed x1, local copies, waits for them, and re-layouts  1.67 us

profile of v4, /device:TPU:1, one launch (start us, length us, event | category | flops | bytes accessed | tf_op | source)
XLA Modules:
  0.0 74.9 jit_solution(16881286813347297725)
XLA Ops:
  0.0 73.2 %layer.1 = bf16[1,128,1024]{2,1,0:T(8,128)(2,1)} custom-call(bf16[1,128,1024]{2,1,0:T(8,128)(2,1)} %x_hbm.1, bf16[16,640]{1,0:T(8,128)(2,1)} %w_hbm.1, bf16[1024,1024]{1,0:T(8,128)(2,1)} %wo_hbm.1, s32[1,1024]{1,0:T(1,128)} %bitcast.2, s32[4,16]{1,0:T(4,128)} %bitcast.3, f32[1,2,16]{2,1,0:T(2,128)} %dec_ref.1), custom_call_target="tpu_custom_call" | custom-call | tf_op jit(solution)/shard_map/layer/pallas_call | solution.py:507
  73.2 1.7 %copy.8 = bf16[1,128,1024]{2,1,0:T(8,128)(2,1)} copy(bf16[1,128,1024]{2,1,0:T(8,128)(2,1)} %layer.1) | data formatting | bytes 524288

commit v5 on v4

--- a/solution.py
+++ b/solution.py
@@ -46,7 +46,7 @@
     xin, win, xbuf, wvb, wqkc, wo, bidb, fmat, qa, ka, va, cc, acc, res,
     sslab, ubuf, sx, tslab, tbuf, cslab, cbuf, stslab, sbuf, sbd, mslab, mbuf,
     dout, dxbuf, pdout, pdbuf,
-    wz_s, wz_r, wx_s, wx_r, wd_s, wd_r, wy_s, wy_r, xg_s, xg_r, sib_s, sib_r,
+    wz_s, wz_r, wx_s, wx_r, wy_s, wy_r, xg_s, xg_r, sib_s, sib_r,
     dx_s, dx_r, pd_s, pd_r, u_s, u_r, t_s, t_r, c_s, c_r, st_s, st_r, m_s, m_r, in_sem,
 ):
     tm, head = lax.axis_index("tm"), lax.axis_index("head")
@@ -62,7 +62,8 @@
     def greet(tm_to, head_to):
         pl.semaphore_signal(barrier, inc=1, device_id=(tm_to, head_to), device_id_type=MESH)
 
-    greet(tm_at(1 - zh, y, x), head)
+    first_half, second_half = zh == 0, zh == 1
+    pl.when(first_half)(lambda: greet(tm_at(1 - zh, y, x), head))
     greet(tm_at(zh, y, lax.rem(x + 2, NX)), head)
     for k in (1, NX - 1):
         greet(tm_at(zh, y, lax.rem(x + k, NX)), head)
@@ -71,7 +72,7 @@
     pl.when(z > 0)(lambda: greet(tm, head - CORES))
     pl.when(z < LINE - 1)(lambda: greet(tm, head + CORES))
     greet(tm, z * CORES + 1 - core)
-    expected = 12 + (z > 0).astype(jnp.int32) + (z < LINE - 1).astype(jnp.int32)
+    expected = 11 + zh + (z > 0).astype(jnp.int32) + (z < LINE - 1).astype(jnp.int32)
 
     loads = [
         pltpu.make_async_copy(src, dst, in_sem.at[i])
@@ -148,9 +149,9 @@
 
     parts = (wvb, wqkc)
 
-    def send_z(c):
+    def send_z(c, go, come):
         ref = parts[c].at[zh, y, x]
-        return [send(ref, ref, wz_s.at[c], wz_r.at[c], tm_at(1 - zh, y, x), head)]
+        return [send(ref, ref, wz_s.at[c], wz_r.at[c], tm_at(1 - zh, y, x), head, go, come)]
 
     def send_x(c, side):
         ref = parts[c].at[zh if side == 0 else 1 - zh, y, x]
@@ -166,33 +167,16 @@
 
     rings = {}
 
-    def send_y(side):
-        ref = wvb.at[zh if side == 0 else 1 - zh, y]
+    def send_y(c, side):
+        ref = parts[c].at[zh if side == 0 else 1 - zh, y]
         return [
-            send(ref, ref, wd_s.at[side, k - 1], wd_r.at[side, k - 1],
+            send(ref, ref, wy_s.at[c, side, k - 1], wy_r.at[c, side, k - 1],
                  tm_at(zh, lax.rem(y + k, NY), x), head)
             for k in (4, 3, 5, 2, 6, 1, 7)
         ]
 
-    def send_ring(side, s):
-        half = zh if side == 0 else 1 - zh
-        rings[side, s] = []
-        for way in range(2) if s < NY // 2 else (side,):
-            held = lax.rem(y - (s - 1) + NY, NY) if way == 0 else lax.rem(y + (s - 1), NY)
-            to = lax.rem(y + (1 if way == 0 else NY - 1), NY)
-            ref = wqkc.at[half, held]
-            rings[side, s].append(
-                send(ref, ref, wy_s.at[side, way, s - 1], wy_r.at[side, way, s - 1],
-                     tm_at(zh, to, x), head)
-            )
-
-    def forward(side, s):
-        take(rings[side, s])
-        if s < NY // 2:
-            send_ring(side, s + 1)
-
     pl.semaphore_wait(barrier, expected)
-    far = send_z(0)
+    far = send_z(0, second_half, first_half)
     own = send_x(0, 0)
     loads[1].wait()
     wide = xin[0].astype(F32)
@@ -204,10 +188,10 @@
             send_line(way, 1, k)
     for k in range(PAIRS):
         send_sib(0, z, k)
-    far_late = send_z(1)
+    far_late = send_z(1, second_half, first_half)
     own_late = send_x(1, 0)
     take(own)
-    direct = send_y(0)
+    direct = send_y(0, 0)
 
     dec = dec_ref[0]
     gi = lax.broadcasted_iota(jnp.int32, (NB, NB), 0)
@@ -228,8 +212,6 @@
             send(dout.at[j], dxbuf.at[x], dx_s.at[k - 1], dx_r.at[k - 1], tm_at(zh, y, j), head)
         )
     take_line(1, 0)
-    take(far)
-    other = send_x(0, 1)
     take_line(1, 1)
 
     ids = jnp.broadcast_to(bid_ref[...].astype(F32), (WIDE, TOKS))
@@ -245,28 +227,48 @@
     fmat[:, 0:NB] = jnp.where(adjacent, 0.0, FAR).astype(BF16)
 
     take_line(1, 2)
-    take(other)
-    direct += send_y(1)
+    take(own_late)
+    late = send_y(1, 0)
     take_line(1, 3)
-    take(far_late)
-    other_late = send_x(1, 1)
-    take_line(2, 0)
-    take_line(2, 1)
-    take(own_late)
-    send_ring(0, 1)
-    take_line(2, 2)
     take(dx)
     prod = dxbuf[0]
     for i in range(1, NX):
         prod = prod * dxbuf[i]
     pdout[...] = prod
     pdbuf[zh, y] = prod
-    take_line(2, 3)
-    take(other_late)
-    send_ring(1, 1)
+    for k in range(CHUNKS):
+        take_line(2, k)
+    take(far)
+    take(send_z(0, first_half, second_half))
+    other = send_x(0, 1)
+    take(far_late)
+    far_late = send_z(1, first_half, second_half)
     take_line(3, 0)
+    take(other)
+    direct += send_y(0, 1)
+    take(far_late)
+    other_late = send_x(1, 1)
     take_line(3, 1)
     take(direct)
+    take(other_late)
+    late += send_y(1, 1)
+
+    def to_group(src_of, dst, ssem, rsem):
+        moves = []
+        for k in range(NY):
+            j = lax.rem(y + k, NY)
+            moves.append(
+                send(src_of(j), dst.at[0, y], ssem.at[1, k], rsem.at[1, k], tm_at(1, j, x), head,
+                     first_half, second_half)
+            )
+        for k in range(1, NY):
+            j = lax.rem(y + k, NY)
+            moves.append(
+                send(src_of(j), dst.at[zh, y], ssem.at[0, k], rsem.at[0, k], tm_at(zh, j, x), head)
+            )
+        return moves
+
+    pd = to_group(lambda j: pdout, pdbuf, pd_s, pd_r)
 
     def project_vb(zz, first):
         rows = pl.ds(pl.multiple_of(zz * ROWS, ROWS), ROWS)
@@ -297,23 +299,6 @@
                 sib[2 * n - 1 + way if n else 0, k].wait_recv()
         project_vb(nearest[n], n == 0)
 
-    first_half, second_half = zh == 0, zh == 1
-
-    def to_group(src_of, dst, ssem, rsem):
-        moves = []
-        for k in range(NY):
-            j = lax.rem(y + k, NY)
-            moves.append(
-                send(src_of(j), dst.at[0, y], ssem.at[1, k], rsem.at[1, k], tm_at(1, j, x), head,
-                     first_half, second_half)
-            )
-        for k in range(1, NY):
-            j = lax.rem(y + k, NY)
-            moves.append(
-                send(src_of(j), dst.at[zh, y], ssem.at[0, k], rsem.at[0, k], tm_at(zh, j, x), head)
-            )
-        return moves
-
     for g in range(NB):
         at = slice(g * WIDE, (g + 1) * WIDE)
         both = jnp.where(low, acc[0:HD, at], acc[HD:WIDE, at])
@@ -325,9 +310,6 @@
             send(sslab.at[j], ubuf.at[x], u_s.at[k - 1], u_r.at[k - 1], tm_at(zh, y, j), head)
         )
     ubuf[x] = sslab[x]
-    forward(0, 1)
-    forward(1, 1)
-    pd = to_group(lambda j: pdout, pdbuf, pd_s, pd_r)
 
     def normed_heads(values):
         square = values * values
@@ -360,8 +342,6 @@
         )
         res[h] = jnp.dot(jnp.exp(score).astype(BF16), va[h], preferred_element_type=F32)
 
-    forward(0, 2)
-    forward(1, 2)
     take(up)
     blocks, owned = NB // NX, 32
     for g in range(blocks):
@@ -376,10 +356,7 @@
             tslab[g * (HD // owned) + n] = piece
     tot = to_group(lambda j: tslab.at[j], tbuf, t_s, t_r)
     tbuf[zh, y] = tslab[y]
-    forward(0, 3)
-    forward(1, 3)
-    take(rings[0, NY // 2])
-    take(rings[1, NY // 2])
+    take(late)
     project_qkc()
     attend(0)
     take(pd)
@@ -497,7 +474,7 @@
         pltpu.VMEM((NZ, NY, 8, WIDE), F32),
     ]
     for shape in (
-        (2,), (2, 2, NX - 1), (2, NY - 1), (2, 2, NY // 2), (2, LINE - 1, CHUNKS),
+        (2,), (2, 2, NX - 1), (2, 2, NY - 1), (2, LINE - 1, CHUNKS),
         (2 * LINE - 1, PAIRS),
         (NX - 1,), (2, NY), (NX - 1,), (2, NY), (NY - 1,), (NX - 1,), (HEADS_AXIS,),
     ):

time: 75 us -> 72.7 us (0.969)
  Pallas kernels: 73.2 us -> 70.8 us
    pallas_call x1, Pallas kernels: 73.2 us -> 70.8 us  [body(): pl.pallas_call(kernel, out_shape=jax.ShapeDtypeStruct((1, LOCAL, D), BF16...]
where the time goes in v5:
time: 72.7 us; the launch traced here: 72.5 us
  Pallas kernels  70.8 us (97%)
  local copies, waits for them, and re-layouts  1.67 us (2%)
    pallas_call x1, Pallas kernels, body(): pl.pallas_call(kernel, out_shape=jax.ShapeDtypeStruct((1, LOCAL, D), BF16...  70.8 us
    unnamed x1, local copies, waits for them, and re-layouts  1.67 us

profile of v5, /device:TPU:1, one launch (start us, length us, event | category | flops | bytes accessed | tf_op | source)
XLA Modules:
  0.0 72.5 jit_solution(6171895102128609238)
XLA Ops:
  0.0 70.8 %layer.1 = bf16[1,128,1024]{2,1,0:T(8,128)(2,1)} custom-call(bf16[1,128,1024]{2,1,0:T(8,128)(2,1)} %x_hbm.1, bf16[16,640]{1,0:T(8,128)(2,1)} %w_hbm.1, bf16[1024,1024]{1,0:T(8,128)(2,1)} %wo_hbm.1, s32[1,1024]{1,0:T(1,128)} %bitcast.2, s32[4,16]{1,0:T(4,128)} %bitcast.3, f32[1,2,16]{2,1,0:T(2,128)} %dec_ref.1), custom_call_target="tpu_custom_call" | custom-call | tf_op jit(solution)/shard_map/layer/pallas_call | solution.py:484
  70.8 1.7 %copy.8 = bf16[1,128,1024]{2,1,0:T(8,128)(2,1)} copy(bf16[1,128,1024]{2,1,0:T(8,128)(2,1)} %layer.1) | data formatting | bytes 524288

commit v6 on v5

--- a/solution.py
+++ b/solution.py
@@ -153,31 +153,29 @@
         ref = parts[c].at[zh, y, x]
         return [send(ref, ref, wz_s.at[c], wz_r.at[c], tm_at(1 - zh, y, x), head, go, come)]
 
-    def send_x(c, side):
+    def send_piece(c, side):
         ref = parts[c].at[zh if side == 0 else 1 - zh, y, x]
-        return [
-            send(ref, ref, wx_s.at[c, side, k - 1], wx_r.at[c, side, k - 1],
-                 tm_at(zh, y, lax.rem(x + k, NX)), head)
-            for k in range(1, NX)
-        ]
-
-    def take(moves):
-        for move in moves:
-            move.wait_recv()
-
-    rings = {}
-
-    def send_y(c, side):
-        ref = parts[c].at[zh if side == 0 else 1 - zh, y]
         return [
             send(ref, ref, wy_s.at[c, side, k - 1], wy_r.at[c, side, k - 1],
                  tm_at(zh, lax.rem(y + k, NY), x), head)
             for k in (4, 3, 5, 2, 6, 1, 7)
         ]
 
+    def take(moves):
+        for move in moves:
+            move.wait_recv()
+
+    def send_bulk(c, side):
+        ref = parts[c].at[zh if side == 0 else 1 - zh, :, x]
+        return [
+            send(ref, ref, wx_s.at[c, side, k - 1], wx_r.at[c, side, k - 1],
+                 tm_at(zh, y, lax.rem(x + k, NX)), head)
+            for k in (2, 1, 3)
+        ]
+
     pl.semaphore_wait(barrier, expected)
     far = send_z(0, second_half, first_half)
-    own = send_x(0, 0)
+    own = send_piece(0, 0)
     loads[1].wait()
     wide = xin[0].astype(F32)
     xbuf[head] = (
@@ -189,9 +187,9 @@
     for k in range(PAIRS):
         send_sib(0, z, k)
     far_late = send_z(1, second_half, first_half)
-    own_late = send_x(1, 0)
+    own_late = send_piece(1, 0)
     take(own)
-    direct = send_y(0, 0)
+    direct = send_bulk(0, 0)
 
     dec = dec_ref[0]
     gi = lax.broadcasted_iota(jnp.int32, (NB, NB), 0)
@@ -228,7 +226,7 @@
 
     take_line(1, 2)
     take(own_late)
-    late = send_y(1, 0)
+    late = send_bulk(1, 0)
     take_line(1, 3)
     take(dx)
     prod = dxbuf[0]
@@ -240,18 +238,18 @@
         take_line(2, k)
     take(far)
     take(send_z(0, first_half, second_half))
-    other = send_x(0, 1)
+    other = send_piece(0, 1)
     take(far_late)
     far_late = send_z(1, first_half, second_half)
     take_line(3, 0)
     take(other)
-    direct += send_y(0, 1)
+    direct += send_bulk(0, 1)
     take(far_late)
-    other_late = send_x(1, 1)
+    other_late = send_piece(1, 1)
     take_line(3, 1)
     take(direct)
     take(other_late)
-    late += send_y(1, 1)
+    late += send_bulk(1, 1)
 
     def to_group(src_of, dst, ssem, rsem):
         moves = []

time: 72.7 us -> 71 us (0.977)
  Pallas kernels: 70.8 us -> 69.1 us
    pallas_call x1, Pallas kernels: 70.8 us -> 69.1 us  [body(): pl.pallas_call(kernel, out_shape=jax.ShapeDtypeStruct((1, LOCAL, D), BF16...]
where the time goes in v6:
time: 71 us; the launch traced here: 70.8 us
  Pallas kernels  69.1 us (97%)
  local copies, waits for them, and re-layouts  1.67 us (2%)
    pallas_call x1, Pallas kernels, body(): pl.pallas_call(kernel, out_shape=jax.ShapeDtypeStruct((1, LOCAL, D), BF16...  69.1 us
    unnamed x1, local copies, waits for them, and re-layouts  1.67 us

profile of v6, /device:TPU:1, one launch (start us, length us, event | category | flops | bytes accessed | tf_op | source)
XLA Modules:
  0.0 70.8 jit_solution(17184849433258537496)
XLA Ops:
  0.0 69.1 %layer.1 = bf16[1,128,1024]{2,1,0:T(8,128)(2,1)} custom-call(bf16[1,128,1024]{2,1,0:T(8,128)(2,1)} %x_hbm.1, bf16[16,640]{1,0:T(8,128)(2,1)} %w_hbm.1, bf16[1024,1024]{1,0:T(8,128)(2,1)} %wo_hbm.1, s32[1,1024]{1,0:T(1,128)} %bitcast.2, s32[4,16]{1,0:T(4,128)} %bitcast.3, f32[1,2,16]{2,1,0:T(2,128)} %dec_ref.1), custom_call_target="tpu_custom_call" | custom-call | tf_op jit(solution)/shard_map/layer/pallas_call | solution.py:482
  69.1 1.7 %copy.8 = bf16[1,128,1024]{2,1,0:T(8,128)(2,1)} copy(bf16[1,128,1024]{2,1,0:T(8,128)(2,1)} %layer.1) | data formatting | bytes 524288

commit v7 on v6

--- a/solution.py
+++ b/solution.py
@@ -266,8 +266,6 @@
             )
         return moves
 
-    pd = to_group(lambda j: pdout, pdbuf, pd_s, pd_r)
-
     def project_vb(zz, first):
         rows = pl.ds(pl.multiple_of(zz * ROWS, ROWS), ROWS)
         tokens = xbuf[pl.ds(zz * CORES, CORES)].reshape(ROWS, D)
@@ -289,9 +287,8 @@
     odd = lax.rem(z, 2)
     nearest = (z, z + 1 - 2 * odd, lax.rem(z + 2, LINE), 3 - z)
     for n in range(LINE):
-        if n == LINE - 1:
-            take_line(3, 2)
-            take_line(3, 3)
+        if 0 < n < LINE - 1:
+            take_line(3, n + 1)
         for way in range(2) if n else (0,):
             for k in range(PAIRS):
                 sib[2 * n - 1 + way if n else 0, k].wait_recv()
@@ -308,6 +305,7 @@
             send(sslab.at[j], ubuf.at[x], u_s.at[k - 1], u_r.at[k - 1], tm_at(zh, y, j), head)
         )
     ubuf[x] = sslab[x]
+    pd = to_group(lambda j: pdout, pdbuf, pd_s, pd_r)
 
     def normed_heads(values):
         square = values * values

time: 71 us -> 70.8 us (level)
  no operation moved by 1% of the time
where the time goes in v7:
time: 70.8 us; the launch traced here: 70.6 us
  Pallas kernels  69 us (97%)
  local copies, waits for them, and re-layouts  1.67 us (2%)
    pallas_call x1, Pallas kernels, body(): pl.pallas_call(kernel, out_shape=jax.ShapeDtypeStruct((1, LOCAL, D), BF16...  69 us
    unnamed x1, local copies, waits for them, and re-layouts  1.67 us

profile of v7, /device:TPU:1, one launch (start us, length us, event | category | flops | bytes accessed | tf_op | source)
XLA Modules:
  0.0 70.6 jit_solution(6622495461763733345)
XLA Ops:
  0.0 69.0 %layer.1 = bf16[1,128,1024]{2,1,0:T(8,128)(2,1)} custom-call(bf16[1,128,1024]{2,1,0:T(8,128)(2,1)} %x_hbm.1, bf16[16,640]{1,0:T(8,128)(2,1)} %w_hbm.1, bf16[1024,1024]{1,0:T(8,128)(2,1)} %wo_hbm.1, s32[1,1024]{1,0:T(1,128)} %bitcast.2, s32[4,16]{1,0:T(4,128)} %bitcast.3, f32[1,2,16]{2,1,0:T(2,128)} %dec_ref.1), custom_call_target="tpu_custom_call" | custom-call | tf_op jit(solution)/shard_map/layer/pallas_call | solution.py:480
  69.0 1.7 %copy.8 = bf16[1,128,1024]{2,1,0:T(8,128)(2,1)} copy(bf16[1,128,1024]{2,1,0:T(8,128)(2,1)} %layer.1) | data formatting | bytes 524288

commit v8 on v7

--- a/solution.py
+++ b/solution.py
@@ -354,7 +354,6 @@
     tbuf[zh, y] = tslab[y]
     take(late)
     project_qkc()
-    attend(0)
     take(pd)
     take(tot)
     own_block = pl.ds(lax.div(y, HD // owned), 1)
@@ -372,6 +371,7 @@
             send(cslab.at[j], cbuf.at[y], c_s.at[k - 1], c_r.at[k - 1], tm_at(zh, j, x), head)
         )
     cbuf[y] = cslab[y]
+    attend(0)
     attend(1)
     take(back)
     for g in range(blocks):

time: 70.8 us -> 70.8 us (level)
  no operation moved by 1% of the time
where the time goes in v8:
time: 70.8 us; the launch traced here: 70.6 us
  Pallas kernels  69 us (97%)
  local copies, waits for them, and re-layouts  1.67 us (2%)
    pallas_call x1, Pallas kernels, body(): pl.pallas_call(kernel, out_shape=jax.ShapeDtypeStruct((1, LOCAL, D), BF16...  69 us
    unnamed x1, local copies, waits for them, and re-layouts  1.67 us

profile of v8, /device:TPU:1, one launch (start us, length us, event | category | flops | bytes accessed | tf_op | source)
XLA Modules:
  0.0 70.6 jit_solution(2760620044601730467)
XLA Ops:
  0.0 69.0 %layer.1 = bf16[1,128,1024]{2,1,0:T(8,128)(2,1)} custom-call(bf16[1,128,1024]{2,1,0:T(8,128)(2,1)} %x_hbm.1, bf16[16,640]{1,0:T(8,128)(2,1)} %w_hbm.1, bf16[1024,1024]{1,0:T(8,128)(2,1)} %wo_hbm.1, s32[1,1024]{1,0:T(1,128)} %bitcast.2, s32[4,16]{1,0:T(4,128)} %bitcast.3, f32[1,2,16]{2,1,0:T(2,128)} %dec_ref.1), custom_call_target="tpu_custom_call" | custom-call | tf_op jit(solution)/shard_map/layer/pallas_call | solution.py:480
  69.0 1.7 %copy.8 = bf16[1,128,1024]{2,1,0:T(8,128)(2,1)} copy(bf16[1,128,1024]{2,1,0:T(8,128)(2,1)} %layer.1) | data formatting | bytes 524288
